TPU v7x, 256 devices: a whole 4x4x8 slice. The times are simulated.
256 devices in a mesh: section: 4 (over y_hi, core), expert: 64 (over z, x, y_lo).
Axes of the slice: x: 4, y: 4 (y_hi: 2, y_lo: 2; y = y_hi * 2 + y_lo), z: 8, core: 2. Of those that a mesh axis runs over, the one named last changes fastest.
Arguments:
- previous: bfloat16 [4, 64, 128, 1024], P('section', 'expert'), may hold values from -6 to 6
- encoder_states: bfloat16 [64, 1024, 1024], P('expert', 'section'), may hold values from -150 to 150
- routes: int32 [4, 64, 128, 2], P('section', 'expert'), may hold values from 0 to 31, all different within a row; in each aligned block of 128 rows (0 to 127, 128 to 255, ..., all dimensions but the last counted through in order) at most 12 rows name the same one
- gate_values: float32 [4, 64, 128, 2], P('section', 'expert'), may hold values from 0.1 to 1
- gain_attn: float32 [4, 1024], P('section'), may hold values from 0.25 to 1.75
- gain_moe: float32 [4, 1024], P('section'), may hold values from 0.25 to 1.75
- query_weight: bfloat16 [4, 1024, 1024], P('section', 'expert'), may hold values from -0.1875 to 0.1875
- key_weight: bfloat16 [4, 1024, 1024], P('section', 'expert'), may hold values from -0.1875 to 0.1875
- value_weight: bfloat16 [4, 1024, 1024], P('section', 'expert'), may hold values from -0.1875 to 0.1875
- out_weight: bfloat16 [4, 1024, 1024], P('section', 'expert'), may hold values from -0.1875 to 0.1875
- expert_gate: bfloat16 [4, 64, 1024, 1408], P('section', 'expert'), may hold values from -0.1875 to 0.1875
- expert_up: bfloat16 [4, 64, 1024, 1408], P('section', 'expert'), may hold values from -0.1875 to 0.1875
- expert_down: bfloat16 [4, 64, 1408, 1024], P('section', 'expert'), may hold values from -0.109375 to 0.109375
Outputs:
- following: bfloat16 [4, 64, 128, 1024], P('section', 'expert')
Inputs may be any that keep to these rules, and one draw needn't show every extreme that they name: In the rows of one index of expert (each section apart) no expert is named by more than 12 routes; the two experts of a token differ.
All inputs are finite; a program needn't handle non-finite values.
Results may differ from a plain program's by a relative error of at most 0.015.
The roundings to bfloat16 on the way count: a program that leaves them out, or rounds other values in their place, can miss the bound.
Values may be sent and summed in bfloat16 or wider, within the bound.
A program may use at most 128 MiB of HBM per device.

v0:
```python
import jax
import jax.numpy as jnp
from jax import lax
from jax.sharding import PartitionSpec as P

HEADS = 16
EXPERTS = 32
CAP = 12


eps = 1e-06


def shifted(value, axis, steps):
    count = lax.axis_size(axis)
    pairs = [(source, (source + steps) % count) for source in range(count)]
    return lax.ppermute(value, axis, pairs)


def rms_scale(x, gain):
    return x * lax.rsqrt(jnp.mean(x * x, axis=-1, keepdims=True) + eps) * gain


def attend(item):
    query, keys, values = item
    head = query.shape[-1]
    scores = jnp.einsum("qhd,khd->hqk", query, keys, preferred_element_type=jnp.float32) * head ** (
        -0.5
    )
    top = jnp.max(scores, axis=-1, keepdims=True)
    expo = jnp.exp(scores - top)
    probs = (expo / jnp.sum(expo, axis=-1, keepdims=True)).astype(jnp.bfloat16)
    context = jnp.einsum("hqk,khd->qhd", probs, values, preferred_element_type=jnp.float32)
    return context.astype(jnp.bfloat16)


def per_device(
    previous,
    encoder_states,
    routes,
    gate_values,
    gain_attn,
    gain_moe,
    query_weight,
    key_weight,
    value_weight,
    out_weight,
    expert_gate,
    expert_up,
    expert_down,
):
    incoming = shifted(previous, "section", 1)
    seq_dev, dec_len, width = (incoming.shape[1], incoming.shape[2], incoming.shape[3])
    head = width // HEADS
    tokens = incoming.reshape(seq_dev * dec_len, width)
    normed = rms_scale(tokens.astype(jnp.float32), gain_attn[0]).astype(jnp.bfloat16)
    enc_len = encoder_states.shape[1] * lax.axis_size("section")
    sources = lax.all_gather(encoder_states, "section", axis=1, tiled=True)
    src_rows = sources.reshape(-1, width)
    query = jnp.dot(
        normed,
        lax.all_gather(query_weight[0], "expert", axis=0, tiled=True),
        preferred_element_type=jnp.float32,
    )
    keys = jnp.dot(
        src_rows,
        lax.all_gather(key_weight[0], "expert", axis=0, tiled=True),
        preferred_element_type=jnp.float32,
    )
    values = jnp.dot(
        src_rows,
        lax.all_gather(value_weight[0], "expert", axis=0, tiled=True),
        preferred_element_type=jnp.float32,
    )
    query = query.astype(jnp.bfloat16)
    keys = keys.astype(jnp.bfloat16).reshape(seq_dev, enc_len, width)
    values = values.astype(jnp.bfloat16).reshape(seq_dev, enc_len, width)
    context = lax.map(
        attend,
        (
            query.reshape(seq_dev, dec_len, HEADS, head),
            keys.reshape(seq_dev, enc_len, HEADS, head),
            values.reshape(seq_dev, enc_len, HEADS, head),
        ),
    )
    context = context.reshape(-1, width)
    attn_out = jnp.dot(
        context,
        lax.all_gather(out_weight[0], "expert", axis=0, tiled=True),
        preferred_element_type=jnp.float32,
    )
    mixed = (tokens.astype(jnp.float32) + attn_out).astype(jnp.bfloat16)
    moe_in = rms_scale(mixed.astype(jnp.float32), gain_moe[0]).astype(jnp.bfloat16)
    flat = routes.reshape(-1)
    onehot = (flat[:, None] == jnp.arange(EXPERTS, dtype=jnp.int32)[None, :]).astype(jnp.int32)
    before = jnp.cumsum(onehot, axis=0) - onehot
    slot = jnp.sum(before * onehot, axis=1)
    position = flat * CAP + slot
    place = (position[None, :] == jnp.arange(EXPERTS * CAP, dtype=jnp.int32)[:, None]).astype(
        jnp.bfloat16
    )
    repeated = jnp.repeat(moe_in, 2, axis=0)
    buffer = (
        jnp.dot(place, repeated, preferred_element_type=jnp.float32)
        .astype(jnp.bfloat16)
        .reshape(EXPERTS, CAP, width)
    )
    split = max(lax.axis_size("expert") // EXPERTS, 1)
    local = expert_gate.shape[1]
    sent = jnp.repeat(buffer, split, axis=0)
    rows = lax.all_to_all(sent, "expert", split_axis=0, concat_axis=0, tiled=True)
    grouped = rows.reshape(-1, local, rows.shape[1], width)
    gated = jnp.einsum(
        "secd,edp->secp", grouped, expert_gate[0], preferred_element_type=jnp.float32
    )
    upper = jnp.einsum("secd,edp->secp", grouped, expert_up[0], preferred_element_type=jnp.float32)
    hidden = (jax.nn.gelu(gated) * upper).astype(jnp.bfloat16)
    partial_value = jnp.einsum(
        "secp,epd->secd", hidden, expert_down[0], preferred_element_type=jnp.float32
    )
    partial_value = partial_value.reshape(rows.shape[0], rows.shape[1], width)
    back = lax.all_to_all(
        partial_value.astype(jnp.bfloat16), "expert", split_axis=0, concat_axis=0, tiled=True
    ).astype(partial_value.dtype)
    expert_out = back.reshape(EXPERTS, split, CAP, width).sum(axis=1).astype(jnp.bfloat16)
    picked = expert_out.reshape(EXPERTS * CAP, width)[position]
    weights = gate_values.reshape(-1)
    moe = (picked.astype(jnp.float32) * weights[:, None]).reshape(-1, 2, width).sum(axis=1)
    result = (mixed.astype(jnp.float32) + moe).astype(jnp.bfloat16)
    return result.reshape(previous.shape)


def solution(mesh):
    in_specs = (
        P("section", "expert", None, None),
        P("expert", "section", None),
        P("section", "expert", None, None),
        P("section", "expert", None, None),
        P("section", None),
        P("section", None),
        P("section", "expert", None),
        P("section", "expert", None),
        P("section", "expert", None),
        P("section", "expert", None),
        P("section", "expert", None, None),
        P("section", "expert", None, None),
        P("section", "expert", None, None),
    )
    out_specs = P("section", "expert", None, None)
    return jax.shard_map(
        per_device, mesh=mesh, in_specs=in_specs, out_specs=out_specs, check_vma=False
    )
```

profile of v0, /device:TPU:16, one launch (start us, length us, event | category | flops | bytes accessed | tf_op | source)
XLA Modules:
  0.0 1387.1 jit_solution(6577001279866574219)
XLA Ops:
  10.0 0.8 copy.25
  12.0 5.5 collective-permute-done
  17.6 293.8 %all-gather.14.cloned.1.call-done = bf16[1,1024,1024]{2,1,0:T(8,128)(2,1)} async-done(((bf16[1,16,1024]{2,1,0:T(8,128)(2,1)}), bf16[1,1024,1024]{2,1,0:T(8,128)(2,1)}) %all-gather.14.cloned.1.call-update) | async-done | bytes 2097168 | tf_op jit(solution)/shard_map/all_gather | solution.py:62
  311.4 2.1 fusion.48
  313.5 0.8 copy.24
  314.3 23.2 %all-gather.10.cloned.1.call-done = bf16[1,1024,1024]{2,1,0:T(8,128)(2,1)} async-done(((bf16[1,256,1024]{2,1,0:T(8,128)(2,1)}), bf16[1,1024,1024]{2,1,0:T(8,128)(2,1)}) %all-gather.10.cloned.1.call-update) | async-done | bytes 2097168 | tf_op jit(solution)/shard_map/all_gather | solution.py:58
  337.5 303.4 %all-gather.16.cloned.1.call-done = bf16[1,1024,1024]{2,1,0:T(8,128)(2,1)} async-done(((bf16[1,16,1024]{2,1,0:T(8,128)(2,1)}), bf16[1,1024,1024]{2,1,0:T(8,128)(2,1)}) %all-gather.16.cloned.1.call-update) | async-done | bytes 2097168 | tf_op jit(solution)/shard_map/all_gather | solution.py:67
  641.0 5.9 fusion.36
  646.9 7.5 fusion.83
  654.4 285.5 %all-gather.12.cloned.1.call-done = bf16[1,1024,1024]{2,1,0:T(8,128)(2,1)} async-done(((bf16[1,16,1024]{2,1,0:T(8,128)(2,1)}), bf16[1,1024,1024]{2,1,0:T(8,128)(2,1)}) %all-gather.12.cloned.1.call-update) | async-done | bytes 2097168 | tf_op jit(solution)/shard_map/all_gather | solution.py:72
  939.9 4.8 fusion.31
  944.7 2.5 fusion.47
  947.2 293.7 %all-gather.18.cloned.1.call-done = bf16[1,1024,1024]{2,1,0:T(8,128)(2,1)} async-done(((bf16[1,16,1024]{2,1,0:T(8,128)(2,1)}), bf16[1,1024,1024]{2,1,0:T(8,128)(2,1)}) %all-gather.18.cloned.1.call-update) | async-done | bytes 2097168 | tf_op jit(solution)/shard_map/all_gather | solution.py:89
  1241.0 2.2 multiply_reduce_fusion.2
  1243.3 1.1 broadcast_in_dim.11
  1244.4 2.0 reshape.147
  1246.4 2.3 convolution_convert_fusion
  1248.8 2.1 reshape.148
  1250.9 1.5 broadcast_in_dim.12
  1252.4 53.8 %all_to_all.10 = bf16[64,12,1024]{2,1,0:T(8,128)(2,1)S(1)} all-to-all(bf16[64,12,1024]{2,1,0:T(8,128)(2,1)S(1)} %bitcast.134), channel_id=1, replica_groups=mesh['section'=4,'expert'=64] {'expert'}, dimensions={0} | all-to-all | bytes 3145728 | tf_op jit(solution)/shard_map/all_to_all | solution.py:111
  1306.2 1.3 copy-done.2
  1307.5 4.4 fusion.19
  1311.9 11.1 fusion.41
  1323.0 3.6 copy.30
  1326.6 9.4 all-to-all-start.1
  1336.5 29.0 %all-to-all-done.1 = bf16[64,12,1024]{2,1,0:T(8,128)(2,1)} async-done(((bf16[64,12,1024]{2,1,0:T(8,128)(2,1)}), bf16[64,12,1024]{2,1,0:T(8,128)(2,1)}, u32[]{:S(2)}, u32[]{:S(2)}) %all-to-all-start.1) | async-done | bytes 1572896 | tf_op jit(solution)/shard_map/all_to_all | solution.py:122
  1365.4 3.4 bitcast_reduce_fusion
  1368.8 2.1 convert_element_type.93
  1370.9 3.6 gather_fusion
  1374.5 2.7 reshape.158
  1377.2 2.6 multiply_reduce_fusion.1
  1379.8 0.8 fusion.68
  (45 shorter events, 5.3 us)
Async XLA Ops:
  6.5 1301.0 %copy-start = (bf16[1,1,1024,1408]{3,2,1,0:T(8,128)(2,1)S(1)}, bf16[1,1,1024,1408]{3,2,1,0:T(8,128)(2,1)}, u32[]{:S(2)}) copy-start(bf16[1,1,1024,1408]{3,2,1,0:T(8,128)(2,1)} %param.23) | copy-start | bytes 8650756
  6.5 304.9 %all-gather.14.cloned.1.call-start = ((), (), s32[]{:S(2)}) async-start(), calls=%async_computation.4 | async-start | bytes 2129920 | tf_op jit(solution)/shard_map/all_gather | solution.py:62
  7.3 330.3 %all-gather.10.cloned.1.call-start = ((), (), s32[]{:S(2)}) async-start(), calls=%async_computation.2 | async-start | bytes 2621440 | tf_op jit(solution)/shard_map/all_gather | solution.py:58
  8.0 633.0 %all-gather.16.cloned.1.call-start = ((), (), s32[]{:S(2)}) async-start(), calls=%async_computation.5 | async-start | bytes 2129920 | tf_op jit(solution)/shard_map/all_gather | solution.py:67
  8.7 931.2 %all-gather.12.cloned.1.call-start = ((), (), s32[]{:S(2)}) async-start(), calls=%async_computation.3 | async-start | bytes 2129920 | tf_op jit(solution)/shard_map/all_gather | solution.py:72
  9.3 1231.6 %all-gather.18.cloned.1.call-start = ((), (), s32[]{:S(2)}) async-start(), calls=%async_computation.6 | async-start | bytes 2129920 | tf_op jit(solution)/shard_map/all_gather | solution.py:89
  9.9 7.6 collective-permute-start
  17.5 629.4 %copy-start.1 = (bf16[1,1,128,1024]{3,2,1,0:T(8,128)(2,1)}, bf16[1,1,128,1024]{3,2,1,0:T(8,128)(2,1)S(1)}, u32[]{:S(2)}) copy-start(bf16[1,1,128,1024]{3,2,1,0:T(8,128)(2,1)S(1)} %collective-permute-done) | copy-start | bytes 786436
  314.3 332.6 %copy-start.3 = (bf16[128,1024]{0,1:T(8,128)(2,1)S(1)}, bf16[128,1024]{0,1:T(8,128)(2,1)}, u32[]{:S(2)}) copy-start(bf16[128,1024]{0,1:T(8,128)(2,1)} %copy.24) | copy-start | bytes 786436
  939.9 4.8 copy-start.7
  947.2 296.0 %copy-start.4 = (f32[1,1024]{1,0:T(1,128)S(1)}, f32[1,1024]{1,0:T(1,128)}, u32[]{:S(2)}) copy-start(f32[1,1024]{1,0:T(1,128)} %param.18) | copy-start | bytes 12292
  1306.2 1.3 copy-start.2
  1326.6 9.4 copy-start.5
  1326.6 9.7 copy-start.6
  1326.6 38.8 %all-to-all-start.1 = ((bf16[64,12,1024]{2,1,0:T(8,128)(2,1)}), bf16[64,12,1024]{2,1,0:T(8,128)(2,1)}, u32[]{:S(2)}, u32[]{:S(2)}) async-start(bf16[64,12,1024]{2,1,0:T(8,128)(2,1)} %copy.30), calls=%async_computation.1 | async-start | bytes 4194304 | tf_op jit(solution)/shard_map/all_to_all | solution.py:122
Sparse Core Ops, SparseCore 0:
  9.1 302.2 all-gather.13
  313.2 24.2 all-gather.9
  339.3 301.5 all-gather.15
  642.6 297.2 all-gather.11
  941.5 299.3 all-gather.17
where the time goes:
time: 1390 us
  waiting for transfers between devices  1240 us (89%)
  blocking collectives  53.8 us (4%)
  matrix products  42.9 us (3%)
  local copies, waits for them, and re-layouts  22.5 us (2%)
    all_gather x1, waiting for transfers between devices, per_device(): lax.all_gather(key_weight[0], 'expert', axis=0, tiled=True)  303 us
    all_gather x1, waiting for transfers between devices, per_device(): lax.all_gather(query_weight[0], 'expert', axis=0, tiled=True)  294 us
    all_gather x1, waiting for transfers between devices, per_device(): lax.all_gather(out_weight[0], 'expert', axis=0, tiled=True)  294 us
    all_gather x1, waiting for transfers between devices, per_device(): lax.all_gather(value_weight[0], 'expert', axis=0, tiled=True)  286 us
    all_to_all x1, blocking collectives, per_device(): lax.all_to_all(sent, 'expert', split_axis=0, concat_axis=0, tiled=True)  53.8 us
    all_to_all x1, waiting for transfers between devices, per_device(): lax.all_to_all(partial_value.astype(jnp.bfloat16), 'expert', split_axis=0...  29 us
  transfers between devices with their start and end apart: 7, of which 7 were waited for; matrix products, arithmetic and copies ran while one was open for 2% of the time, Pallas kernels for 0%

commit v1 on v0

v1 whole, which is shorter than its diff:
```python
import functools

import jax
import jax.numpy as jnp
import numpy as np
from jax import lax
from jax.experimental import pallas as pl
from jax.experimental.pallas import tpu as pltpu
from jax.sharding import PartitionSpec as P

EXPERTS = 32
CAP = 12
NZ, NX, NY = 8, 4, 4
DEC, ENC, D = 128, 1024, 1024
HALF = D // 2
QUART = D // 4
PIECE = 1408
SLOTS = EXPERTS * CAP
EPS = 1e-06
MESH = pl.DeviceIdType.MESH
BF, F32 = jnp.bfloat16, jnp.float32


def place_of():
    s, e = lax.axis_index("section"), lax.axis_index("expert")
    return e // 8, (e // 2) % NX, (s // 2) * 2 + e % 2, s % 2


def device(z, x, y, core):
    return ((y // 2) * 2 + core, (z * NX + x) * 2 + y % 2)


class Sems:
    def __init__(self, ref):
        self.ref, self.used = ref, 0

    def take(self, count=1):
        first = self.used
        self.used += count
        return first


def rms(x, gain):
    return x * lax.rsqrt(jnp.mean(x * x, axis=-1, keepdims=True) + EPS) * gain


def dot(a, b):
    return jnp.dot(a, b, preferred_element_type=F32)


SEMS_A = 160


def attention_kernel(prev, enc, wq, wk, wv, wo, gain, out, E, W, T, K, V, Q, C, MX, H, GM, ssem, rsem):
    z, x, y, b = place_of()
    a, yhi = y % 2, y // 2
    zp, zm = (z + 1) % NZ, (z + NZ - 1) % NZ
    xp, xm, xo = (x + 1) % NX, (x + NX - 1) % NX, (x + 2) % NX
    yp, ym, yo = (y + 1) % NY, (y + NY - 1) % NY, (y + 2) % NY
    mate = device(z, x, y, 1 - b)
    take = Sems(rsem).take
    pending = []

    bar = pltpu.get_barrier_semaphore()
    shift_src = (y + 3) % NY
    greet = [
        mate,
        device(z, x, y + 1 - 2 * a, b),
        device(z, x, y + 1 - 2 * a, 1 - b),
        device(zp, x, y, b),
        device(zm, x, y, b),
        device(z, xp, y, b),
        device(z, xm, y, b),
        device(z, xo, y, b),
        device(z, x, yp, b),
        device(z, x, ym, b),
        device(z, x, (shift_src // 2) * 2 + b, shift_src % 2),
    ]
    for other in greet:
        pl.semaphore_signal(bar, inc=1, device_id=other, device_id_type=MESH)
    pl.semaphore_wait(bar, len(greet))

    def remote(src, dst, i, to):
        return pltpu.make_async_remote_copy(
            src_ref=src, dst_ref=dst, send_sem=ssem.at[i], recv_sem=rsem.at[i],
            device_id=to, device_id_type=MESH,
        )

    def send(src, dst, i, to):
        copy = remote(src, dst, i, to)
        copy.start()
        pending.append(copy.wait_send)

    def arrived(dst, i):
        remote(dst, dst, i, mate).wait_recv()

    def send_or_keep(src, dst, i, to, here):
        @pl.when(here)
        def _():
            pltpu.make_async_copy(src, dst, rsem.at[i]).start()

        @pl.when(jnp.logical_not(here))
        def _():
            remote(src, dst, i, to).start()

        def wait():
            @pl.when(jnp.logical_not(here))
            def _():
                remote(src, dst, i, to).wait_send()

        pending.append(wait)

    weights = (wk, wq, wv, wo)
    quad = [take(4) for _ in weights]
    for n, w in enumerate(weights):
        for h in (0, 1):
            src = w.at[:, pl.ds(h * HALF, HALF)]
            dst = W.at[n, z, x, pl.ds(a * 16, 16), :]
            here = jnp.logical_and(a == h, b == h)
            i = quad[n] + 2 * h + a

            @pl.when(here)
            def _():
                pltpu.make_async_copy(src, dst, rsem.at[i]).start()

            @pl.when(jnp.logical_not(here))
            def _():
                remote(src, dst, i, device(z, x, yhi * 2 + b, h)).start()

            def wait(src=src, dst=dst, i=i, h=h, here=here):
                @pl.when(jnp.logical_not(here))
                def _():
                    remote(src, dst, i, device(z, x, yhi * 2 + b, h)).wait_send()

            pending.append(wait)

    gain_mate = take()
    send(gain, GM, gain_mate, mate)

    tok, tok_mate = take(), take()
    send(prev, T.at[a], tok, device(z, x, (yhi * 2 + b + 1) % NY, a))

    def slot(yy, core):
        return E.at[yy % 2, (yy // 2) * 2 + core]

    def half(ref, i):
        return ref.at[pl.ds(i * 128, 128), :]

    e_p, e_m, e_op, e_om = take(2), take(2), take(), take()
    c_own, c_p, c_m, c_o = take(), take(2), take(2), take(2)
    for i in (0, 1):
        send(half(enc, i), half(slot(y, b), i), e_p + i, device(z, x, yp, b))
        send(half(enc, 1 - i), half(slot(y, b), 1 - i), e_m + 1 - i, device(z, x, ym, b))
    own = pltpu.make_async_copy(enc, slot(y, b), rsem.at[take()])
    own.start()
    send(enc, slot(y, b), c_own, mate)

    left, right = pl.ds(0, 256), pl.ds(256, 256)
    ax = [take(3) for _ in weights]
    az = [take(8) for _ in weights]
    bz = [take(8) for _ in weights]
    bx = [take(4) for _ in weights]

    def zz(d):
        return (z + d + NZ) % NZ

    def xx(d):
        return (x + d + NX) % NX

    def a_block(n, zi, xs=None):
        return W.at[n, zi, :, :, left] if xs is None else W.at[n, zi, pl.ds(xs, 2), :, left]

    def b_block(n, zi, rows=None):
        if rows is None:
            return W.at[n, zi, x, :, right]
        return W.at[n, zi, x, pl.ds(rows, 16), right]

    def b_slab(n, xi, zs=None):
        return W.at[n, :, xi, :, right] if zs is None else W.at[n, pl.ds(zs, 4), xi, :, right]

    def ring_z(block, sem, n, step):
        if step > 1:
            arrived(block(n, zz(1 - step)), sem[n] + 2 * (step - 2))
            arrived(block(n, zz(step - 1)), sem[n] + 2 * (step - 2) + 1)
        up, down = device(zp, x, y, b), device(zm, x, y, b)
        i = sem[n] + 2 * (step - 1)
        if step < 4:
            send(block(n, zz(1 - step)), block(n, zz(1 - step)), i, up)
            send(block(n, zz(step - 1)), block(n, zz(step - 1)), i + 1, down)
        else:
            lo, hi = (0, 2) if block is a_block else (0, 16)
            send(block(n, zz(-3), lo), block(n, zz(-3), lo), i, up)
            send(block(n, zz(3), hi), block(n, zz(3), hi), i + 1, down)

    def ring_z_end(block, sem, n):
        lo, hi = (0, 2) if block is a_block else (0, 16)
        arrived(block(n, zz(4), lo), sem[n] + 6)
        arrived(block(n, zz(4), hi), sem[n] + 7)

    def s1(n):
        mine = W.at[n, z, x]
        for i in (0, 1):
            arrived(mine.at[pl.ds(16 * i, 16), :], quad[n] + 2 * b + i)
        piece = W.at[n, z, x, :, left]
        for i, xi in enumerate((xp, xm, xo)):
            send(piece, piece, ax[n] + i, device(z, xi, y, b))
        ring_z(b_block, bz, n, 1)

    def s2(n):
        for i, xi in enumerate((xm, xp, xo)):
            arrived(W.at[n, z, xi, :, left], ax[n] + i)
        ring_z(a_block, az, n, 1)
        ring_z(b_block, bz, n, 2)

    def s3(n):
        ring_z(b_block, bz, n, 3)
        ring_z(a_block, az, n, 2)

    def s4(n):
        ring_z(b_block, bz, n, 4)
        ring_z(a_block, az, n, 3)

    def s5(n):
        ring_z_end(b_block, bz, n)
        send(b_slab(n, x), b_slab(n, x), bx[n], device(z, xp, y, b))
        send(b_slab(n, x), b_slab(n, x), bx[n] + 1, device(z, xm, y, b))
        ring_z(a_block, az, n, 4)

    def s6(n):
        arrived(b_slab(n, xm), bx[n])
        arrived(b_slab(n, xp), bx[n] + 1)
        send(b_slab(n, xm, 0), b_slab(n, xm, 0), bx[n] + 2, device(z, xp, y, b))
        send(b_slab(n, xp, 4), b_slab(n, xp, 4), bx[n] + 3, device(z, xm, y, b))

    def s7(n):
        ring_z_end(a_block, az, n)
        arrived(b_slab(n, xo, 0), bx[n] + 2)
        arrived(b_slab(n, xo, 4), bx[n] + 3)

    def e1():
        arrived(T.at[b], tok)
        send(T.at[b], T.at[b], tok_mate, mate)

    def e2():
        arrived(half(slot(ym, b), 0), e_p)
        send(half(slot(ym, b), 0), half(slot(ym, b), 0), e_op, device(z, x, yp, b))
        send(half(slot(ym, b), 0), half(slot(ym, b), 0), c_m, mate)
        arrived(half(slot(yp, b), 1), e_m + 1)
        send(half(slot(yp, b), 1), half(slot(yp, b), 1), e_om, device(z, x, ym, b))
        send(half(slot(yp, b), 1), half(slot(yp, b), 1), c_p + 1, mate)

    def e3():
        arrived(half(slot(ym, b), 1), e_p + 1)
        send(half(slot(ym, b), 1), half(slot(ym, b), 1), c_m + 1, mate)
        arrived(half(slot(yp, b), 0), e_m)
        send(half(slot(yp, b), 0), half(slot(yp, b), 0), c_p, mate)

    def e4():
        arrived(half(slot(yo, b), 0), e_op)
        send(half(slot(yo, b), 0), half(slot(yo, b), 0), c_o, mate)
        arrived(half(slot(yo, b), 1), e_om)
        send(half(slot(yo, b), 1), half(slot(yo, b), 1), c_o + 1, mate)

    stages = (s1, s2, s3, s4, s5, s6, s7)
    extra = {2: e1, 4: e2, 6: e3, 9: e4}
    for time in range(len(stages) + 3):
        for n in range(4):
            if 0 <= time - n < len(stages):
                stages[time - n](n)
        if time in extra:
            extra[time]()

    own.wait()
    arrived(T.at[1 - b], tok_mate)
    arrived(slot(y, 1 - b), c_own)
    for i in (0, 1):
        arrived(half(slot(ym, 1 - b), i), c_m + i)
        arrived(half(slot(yp, 1 - b), i), c_p + i)
        arrived(half(slot(yo, 1 - b), i), c_o + i)

    def weight(n):
        return W[n].reshape(D, HALF)

    arrived(GM, gain_mate)
    scale = jnp.where(a == b, gain[...], GM[...])
    normed = rms(T[...].reshape(2 * DEC, D).astype(F32), scale).astype(BF)
    Q[...] = dot(normed, weight(1)).astype(BF)

    @pl.loop(0, 8)
    def _(i):
        block = E[i // 4, i % 4]
        K[pl.ds(i * 256, 256), :] = dot(block, weight(0)).astype(BF)
        V[pl.ds(i * 256, 256), :] = dot(block, weight(2)).astype(BF)

    lane = lax.broadcasted_iota(jnp.int32, (DEC, 128), 1)

    @pl.loop(0, 8)
    def _(i):
        seq, pair = i // 4, i % 4
        columns = pl.ds(pl.multiple_of(pair * 128, 128), 128)
        rows = pl.ds(seq * DEC, DEC)
        keys = pl.ds(seq * ENC, ENC)
        q = Q[rows, columns]
        both = jnp.concatenate(
            [jnp.where(lane < 64, q, 0).astype(BF), jnp.where(lane >= 64, q, 0).astype(BF)], axis=0
        )
        scores = lax.dot_general(
            both, K[keys, columns], (((1,), (1,)), ((), ())), preferred_element_type=F32
        )
        top = jnp.max(scores, axis=-1, keepdims=True)
        expo = jnp.exp((scores - top) * 0.125)
        probs = (expo * (1.0 / jnp.sum(expo, axis=-1, keepdims=True))).astype(BF)
        mixed2 = dot(probs, V[keys, columns])
        C[b, rows, columns] = jnp.where(lane < 64, mixed2[:DEC], mixed2[DEC:]).astype(BF)

    ctx = take()
    send(C.at[b], C.at[b], ctx, mate)
    arrived(C.at[1 - b], ctx)
    wout = weight(3)
    attn = dot(C[0], wout[:HALF]) + dot(C[1], wout[HALF:])
    mine = pl.ds(pl.multiple_of(b * HALF, HALF), HALF)
    for c in (0, 1):
        MX[c] = (T[c, :, mine].astype(F32) + attn[c * DEC : (c + 1) * DEC]).astype(BF)

    home = take(4)
    for c in (0, 1):
        src, dst = MX.at[c], H.at[b]
        i = home + 2 * c + b
        here = jnp.logical_and(a == c, b == c)
        to = device(z, x, yhi * 2 + c, a)
        send_or_keep(src, dst, i, to, here)
    for h in (0, 1):
        arrived(H.at[h], home + 2 * a + h)
    for h in (0, 1):
        out[:, h * HALF : (h + 1) * HALF] = H[h]
    for wait in pending:
        wait()


def attention(prev, enc, wq, wk, wv, wo, gain):
    vmem = pl.BlockSpec(memory_space=pltpu.VMEM)
    return pl.pallas_call(
        attention_kernel,
        name="attention",
        out_shape=jax.ShapeDtypeStruct((DEC, D), BF),
        in_specs=[vmem] * 7,
        out_specs=vmem,
        scratch_shapes=[
            pltpu.VMEM((2, 4, 256, D), BF),
            pltpu.VMEM((4, NZ, NX, 32, HALF), BF),
            pltpu.VMEM((2, DEC, D), BF),
            pltpu.VMEM((2 * ENC, HALF), BF),
            pltpu.VMEM((2 * ENC, HALF), BF),
            pltpu.VMEM((2 * DEC, HALF), BF),
            pltpu.VMEM((2, 2 * DEC, HALF), BF),
            pltpu.VMEM((2, DEC, HALF), BF),
            pltpu.VMEM((2, DEC, HALF), BF),
            pltpu.VMEM((1, D), F32),
            pltpu.SemaphoreType.DMA((SEMS_A,)),
            pltpu.SemaphoreType.DMA((SEMS_A,)),
        ],
        compiler_params=pltpu.CompilerParams(
            collective_id=1, has_side_effects=True, vmem_limit_bytes=48 << 20
        ),
    )(prev, enc, wq, wk, wv, wo, gain)


def moe_kernel(mixed, gain, routes, routes_t, gates, spread, gather, wg, wu, wd, out,
               G, U, DN, B0, BUF, X, XR, HID, OWN, PS, PX, RB, R, RR,
               wsem, dsend, drecv, fsend, frecv, psem, rsend, rrecv):
    z, x, y, b = place_of()
    sec, exp = lax.axis_index("section"), lax.axis_index("expert")
    here, a = exp // 2, exp % 2
    partner = (sec, exp + 1 - 2 * a)

    loads = [
        pltpu.make_async_copy(src, dst, wsem.at[i])
        for i, (src, dst) in enumerate(((wg, G), (wu, U), (wd, DN)))
    ]
    for load in loads:
        load.start()

    def at(k, sign):
        zk, xk = k // NX, k % NX
        return ((z + sign * zk + NZ) % NZ) * NX + (x + sign * xk + NX) % NX

    bar = pltpu.get_barrier_semaphore()

    @pl.loop(1, 32)
    def _(k):
        pl.semaphore_signal(bar, inc=1, device_id=(sec, at(k, -1) * 2 + a), device_id_type=MESH)

    pl.semaphore_signal(bar, inc=1, device_id=partner, device_id_type=MESH)

    def remote(src, dst, s, r, to):
        return pltpu.make_async_remote_copy(
            src_ref=src, dst_ref=dst, send_sem=s, recv_sem=r, device_id=to, device_id_type=MESH
        )

    moe_in = rms(mixed[...].astype(F32), gain[...]).astype(BF)
    expert_r = lax.broadcasted_iota(jnp.int32, (EXPERTS, DEC), 0)
    hot = [(expert_r == routes_t[k : k + 1, :]).astype(F32) for k in (0, 1)]
    t0 = lax.broadcasted_iota(jnp.int32, (DEC, DEC), 0)
    t1 = lax.broadcasted_iota(jnp.int32, (DEC, DEC), 1)
    count = dot((hot[0] + hot[1]).astype(BF), (t0 < t1).astype(BF))
    slot_id = lax.broadcasted_iota(jnp.int32, (SLOTS, DEC), 0)
    place = jnp.zeros((SLOTS, DEC), F32)
    for k in (0, 1):
        slot = jnp.sum(count * hot[k], axis=0, keepdims=True).astype(jnp.int32)
        position = routes_t[k : k + 1, :] * CAP + slot
        place = place + (slot_id == position).astype(F32)
    B0[...] = dot(place.astype(BF), moe_in).astype(BF)

    def to_blocks(src, dst):
        @pl.loop(0, 8)
        def _(g):
            rows = pl.ds(g * 48, 48)
            stacked = jnp.concatenate(
                [src[rows, q * QUART : (q + 1) * QUART] for q in range(4)], axis=0
            )
            dst[pl.ds(g * 4, 4)] = dot(spread[...], stacked).astype(BF).reshape(4, 48, QUART)

    def to_rows(src, dst, first):
        @pl.loop(0, 8)
        def _(g):
            stacked = dot(gather[...], src[pl.ds(g * 4, 4)].reshape(192, QUART)).astype(BF)
            for q in range(4):
                dst[pl.ds(first + g * 48, 48), q * QUART : (q + 1) * QUART] = stacked[
                    q * 48 : (q + 1) * 48
                ]

    to_blocks(B0, BUF)
    pl.semaphore_wait(bar, 32)

    @pl.loop(1, 32)
    def _(k):
        to = at(k, 1)
        remote(BUF.at[to], X.at[0, here], dsend.at[k], drecv.at[k], (sec, to * 2 + a)).start()

    X[0, here] = BUF[here]

    @pl.loop(0, 32)
    def _(k):
        src = at(k, -1)

        @pl.when(k > 0)
        def _():
            remote(X.at[0, src], X.at[0, src], dsend.at[k], drecv.at[k], partner).wait_recv()

        remote(X.at[0, src], X.at[1, src], fsend.at[k], frecv.at[k], partner).start()

    @pl.loop(0, 32)
    def _(k):
        src = at(k, -1)
        remote(X.at[1, src], X.at[1, src], fsend.at[k], frecv.at[k], partner).wait()

    to_rows(X.at[0], XR, 0)
    to_rows(X.at[1], XR, SLOTS)
    for load in loads:
        load.wait()

    def expert(first):
        rows = XR[pl.ds(first, 192), :]
        gated, upper = dot(rows, G[...]), dot(rows, U[...])
        HID[...] = (jax.nn.gelu(gated) * upper).astype(BF)
        return dot(HID[...], DN[...])

    @pl.loop(0, 2)
    def _(i):
        PS[pl.ds(i * 192, 192), :] = expert(SLOTS + i * 192).astype(BF)

    swap = remote(PS, PX, psem.at[0], psem.at[1], partner)
    swap.start()

    @pl.loop(0, 2)
    def _(i):
        OWN[pl.ds(i * 192, 192), :] = expert(i * 192)

    swap.wait()
    B0[...] = (OWN[...] + PX[...].astype(F32)).astype(BF)
    to_blocks(B0, RB)

    @pl.loop(1, 32)
    def _(k):
        to = at(k, 1)
        remote(RB.at[to], R.at[here], rsend.at[k], rrecv.at[k], (sec, to * 2 + a)).start()

    R[here] = RB[here]

    expert_c = lax.broadcasted_iota(jnp.int32, (DEC, EXPERTS), 1)
    hot = [(expert_c == routes[:, k : k + 1]).astype(F32) for k in (0, 1)]
    count = dot((t1 < t0).astype(BF), (hot[0] + hot[1]).astype(BF))
    slot_id = lax.broadcasted_iota(jnp.int32, (DEC, SLOTS), 1)
    picks = []
    for k in (0, 1):
        slot = jnp.sum(count * hot[k], axis=1, keepdims=True).astype(jnp.int32)
        picks.append((slot_id == routes[:, k : k + 1] * CAP + slot).astype(F32).astype(BF))

    @pl.loop(1, 32)
    def _(k):
        src = at(k, -1)
        remote(R.at[src], R.at[src], rsend.at[k], rrecv.at[k], partner).wait()
        remote(BUF.at[src], BUF.at[src], dsend.at[k], drecv.at[k], partner).wait_send()

    to_rows(R, RR, 0)
    total = mixed[...].astype(F32)
    moe = [dot(picks[k], RR[...]) * gates[:, k : k + 1] for k in (0, 1)]
    out[...] = (total + (moe[0] + moe[1])).astype(BF)


def spread_matrix():
    m = np.zeros((192, 192), np.float32)
    for s in range(4):
        for q in range(4):
            for c in range(CAP):
                m[s * 48 + q * 12 + c, q * 48 + s * 12 + c] = 1
    return m


def experts(mixed, gain, routes, gates, wg, wu, wd):
    vmem, hbm = pl.BlockSpec(memory_space=pltpu.VMEM), pl.BlockSpec(memory_space=pl.ANY)
    spread = spread_matrix()
    dma = pltpu.SemaphoreType.DMA
    return pl.pallas_call(
        moe_kernel,
        name="experts",
        out_shape=jax.ShapeDtypeStruct((DEC, D), BF),
        in_specs=[vmem] * 7 + [hbm] * 3,
        out_specs=vmem,
        scratch_shapes=[
            pltpu.VMEM((D, PIECE), BF),
            pltpu.VMEM((D, PIECE), BF),
            pltpu.VMEM((PIECE, D), BF),
            pltpu.VMEM((SLOTS, D), BF),
            pltpu.VMEM((32, 48, QUART), BF),
            pltpu.VMEM((2, 32, 48, QUART), BF),
            pltpu.VMEM((2 * SLOTS, D), BF),
            pltpu.VMEM((192, PIECE), BF),
            pltpu.VMEM((SLOTS, D), F32),
            pltpu.VMEM((SLOTS, D), BF),
            pltpu.VMEM((SLOTS, D), BF),
            pltpu.VMEM((32, 48, QUART), BF),
            pltpu.VMEM((32, 48, QUART), BF),
            pltpu.VMEM((SLOTS, D), BF),
            dma((3,)),
            dma((32,)),
            dma((32,)),
            dma((32,)),
            dma((32,)),
            dma((2,)),
            dma((32,)),
            dma((32,)),
        ],
        compiler_params=pltpu.CompilerParams(
            collective_id=2, has_side_effects=True, vmem_limit_bytes=56 << 20
        ),
    )(mixed, gain, routes, routes.T, gates, jnp.asarray(spread, BF), jnp.asarray(spread.T, BF), wg, wu, wd)


def per_device(previous, encoder_states, routes, gate_values, gain_attn, gain_moe, query_weight,
               key_weight, value_weight, out_weight, expert_gate, expert_up, expert_down):
    mixed = attention(
        previous[0, 0], encoder_states[0], query_weight[0], key_weight[0], value_weight[0],
        out_weight[0], gain_attn,
    )
    result = experts(
        mixed, gain_moe, routes[0, 0], gate_values[0, 0], expert_gate[0, 0], expert_up[0, 0],
        expert_down[0, 0],
    )
    return result.reshape(previous.shape)


def solution(mesh):
    in_specs = (
        P("section", "expert", None, None),
        P("expert", "section", None),
        P("section", "expert", None, None),
        P("section", "expert", None, None),
        P("section", None),
        P("section", None),
        P("section", "expert", None),
        P("section", "expert", None),
        P("section", "expert", None),
        P("section", "expert", None),
        P("section", "expert", None, None),
        P("section", "expert", None, None),
        P("section", "expert", None, None),
    )
    out_specs = P("section", "expert", None, None)
    return jax.shard_map(
        per_device, mesh=mesh, in_specs=in_specs, out_specs=out_specs, check_vma=False
    )
```

time: 1390 us -> 174 us (0.13)
  the two profiles are of different devices: /device:TPU:16 before, /device:TPU:64 now
where the time goes in v1:
time: 174 us; the launch traced here: 173 us
  Pallas kernels  162 us (93%)
  local copies, waits for them, and re-layouts  10.9 us (6%)
    pallas_call x1, Pallas kernels, experts(): pl.pallas_call(moe_kernel, name='experts', out_shape=jax.ShapeDtypeStruct...  89.1 us
    pallas_call x1, Pallas kernels, attention(): pl.pallas_call(attention_kernel, name='attention', out_shape=jax.ShapeDty...  73.3 us
    unnamed x18, local copies, waits for them, and re-layouts  9.47 us

profile of v1, /device:TPU:64, one launch (start us, length us, event | category | flops | bytes accessed | tf_op | source)
XLA Modules:
  0.0 173.4 jit_solution(1086385241376398573)
XLA Ops:
  0.0 1.4 copy.16
  1.4 1.4 copy.17.routes
  2.8 0.0 copy-start.1
  2.8 1.0 copy-done.1
  3.8 0.0 copy-start.2
  3.8 0.9 copy-done.2
  4.8 0.0 copy-start.3
  4.8 0.8 copy-done.3
  5.6 0.0 copy-start.4
  5.6 0.8 copy-done.4
  6.3 0.0 copy-start.5
  6.3 0.8 copy-done.5
  7.1 0.0 copy-start.6
  7.1 0.8 copy-done.6
  7.8 0.0 copy-start.7
  7.8 0.7 copy-done.7
  8.5 73.3 %attention.1.mixed = bf16[128,1024]{1,0:T(8,128)(2,1)S(1)} custom-call(bf16[128,1024]{1,0:T(8,128)(2,1)S(1)} %bitcast.15, bf16[256,1024]{1,0:T(8,128)(2,1)S(1)} %bitcast.14, bf16[16,1024]{1,0:T(8,128)(2,1)S(1)} %bitcast.16, bf16[16,1024]{1,0:T(8,128)(2,1)S(1)} %bitcast.17, bf16[16,1024]{1,0:T(8,128)(2,1)S(1)} %bitcast.18, bf16[16,1024]{1,0:T(8,128)(2,1)S(1)} %bitcast.19, ...), custom_call_target="tpu_custom_call" | custom-call | tf_op jit(solution)/shard_map/attention/pallas_call | solution.py:342
  81.9 0.0 copy-start
  81.9 0.7 copy-done
  82.6 89.1 %experts.1 = bf16[128,1024]{1,0:T(8,128)(2,1)} custom-call(bf16[128,1024]{1,0:T(8,128)(2,1)} %copy-done, f32[1,1024]{1,0:T(1,128)} %gain.3, s32[128,2]{1,0:T(8,128)} %copy.17.routes, s32[2,128]{1,0:T(2,128)} %bitcast.26, f32[128,2]{1,0:T(8,128)} %bitcast.24, bf16[192,192]{1,0:T(8,128)(2,1)} %constant.2.clone.spread.gather, ...), custom_call_target="tpu_custom_call" | custom-call | tf_op jit(solution)/shard_map/experts/pallas_call | solution.py:524
  171.7 1.7 copy.19
Async XLA Ops:
  2.8 1.0 copy-start.1
  3.8 0.9 copy-start.2
  4.8 0.8 copy-start.3
  5.6 0.8 copy-start.4
  6.3 0.8 copy-start.5
  7.1 0.8 copy-start.6
  7.8 0.7 copy-start.7
  81.9 0.7 copy-start

commit v2 on v1

v2 whole, which is shorter than its diff:
```python
import functools

import jax
import jax.numpy as jnp
import numpy as np
from jax import lax
from jax.experimental import pallas as pl
from jax.experimental.pallas import tpu as pltpu
from jax.sharding import PartitionSpec as P

EXPERTS = 32
CAP = 12
NZ, NX, NY = 8, 4, 4
DEC, ENC, D = 128, 1024, 1024
HALF = D // 2
QUART = D // 4
PIECE = 1408
SLOTS = EXPERTS * CAP
EPS = 1e-06
MESH = pl.DeviceIdType.MESH
BF, F32 = jnp.bfloat16, jnp.float32


def place_of():
    s, e = lax.axis_index("section"), lax.axis_index("expert")
    return e // 8, (e // 2) % NX, (s // 2) * 2 + e % 2, s % 2


def device(z, x, y, core):
    return ((y // 2) * 2 + core, (z * NX + x) * 2 + y % 2)


class Sems:
    def __init__(self, ref):
        self.ref, self.used = ref, 0

    def take(self, count=1):
        first = self.used
        self.used += count
        return first


def rms(x, gain):
    return x * lax.rsqrt(jnp.mean(x * x, axis=-1, keepdims=True) + EPS) * gain


def dot(a, b):
    return jnp.dot(a, b, preferred_element_type=F32)


SEMS_A = 180


GROUPS = (
    (
        (("k", 0), ("k", 1), ("v", 0), ("v", 1), ("q", 0), ("q", 1)),
        (("k", 2), ("k", 3), ("v", 2), ("v", 3), ("q", 2), ("q", 3)),
    ),
    (
        (("o", 0),),
        (("o", 1), ("o", 2), ("o", 3)),
    ),
)


def make_plan(behind, places):
    plan = []
    for time in range(1, 9 + behind):
        plan += [f"s{time - g * behind} {g}" for g in (0, 1) if 1 <= time - g * behind <= 8]
        plan += places.get(time, [])
    return plan + places.get(0, [])


PLAN = make_plan(
    2,
    {
        5: ["e2"],
        7: ["e3", "e1"],
        8: ["e4", "ck 0", "ck 1"],
        9: ["ck 3", "ck 2", "cv 0", "cv 1", "cv 3", "cv 2", "cq", "at 0"],
        10: ["at 1"],
    },
)


def attention_kernel(plan, prev, enc, wq, wk, wv, wo, gain, out, E, WA0, WB0, WA1, WB1, T, K, V, Q, C, MX, H, GM, GO, S, ssem, rsem):
    WA, WB = (WA0, WA1), (WB0, WB1)
    z, x, y, b = place_of()
    a, yhi = y % 2, y // 2
    zp, zm = (z + 1) % NZ, (z + NZ - 1) % NZ
    xp, xm, xo = (x + 1) % NX, (x + NX - 1) % NX, (x + 2) % NX
    yp, ym, yo = (y + 1) % NY, (y + NY - 1) % NY, (y + 2) % NY
    mate = device(z, x, y, 1 - b)
    take = Sems(rsem).take
    pending = []

    bar = pltpu.get_barrier_semaphore()
    shift_src = (y + 3) % NY
    greet = [
        mate,
        device(z, x, y + 1 - 2 * a, b),
        device(z, x, y + 1 - 2 * a, 1 - b),
        device(zp, x, y, b),
        device(zm, x, y, b),
        device(z, xp, y, b),
        device(z, xm, y, b),
        device(z, xo, y, b),
        device(z, x, yp, b),
        device(z, x, ym, b),
        device(z, x, (shift_src // 2) * 2 + b, shift_src % 2),
    ]
    for other in greet:
        pl.semaphore_signal(bar, inc=1, device_id=other, device_id_type=MESH)
    pl.semaphore_wait(bar, len(greet))

    def remote(src, dst, i, to):
        return pltpu.make_async_remote_copy(
            src_ref=src, dst_ref=dst, send_sem=ssem.at[i], recv_sem=rsem.at[i],
            device_id=to, device_id_type=MESH,
        )

    def send(src, dst, i, to):
        copy = remote(src, dst, i, to)
        copy.start()
        pending.append(copy.wait_send)

    def arrived(dst, i):
        remote(dst, dst, i, mate).wait_recv()

    def send_or_keep(src, dst, i, to, here):
        @pl.when(here)
        def _():
            pltpu.make_async_copy(src, dst, rsem.at[i]).start()

        @pl.when(jnp.logical_not(here))
        def _():
            remote(src, dst, i, to).start()

        def wait():
            @pl.when(jnp.logical_not(here))
            def _():
                remote(src, dst, i, to).wait_send()

        pending.append(wait)

    names = "kvqo"
    weights = dict(k=wk, v=wv, q=wq, o=wo)
    quad = [take(4) for _ in names]
    for n, name in enumerate(names):
        for h in (0, 1):
            send_or_keep(
                weights[name].at[:, pl.ds(h * HALF, HALF)], S.at[n, a], quad[n] + 2 * h + a,
                device(z, x, yhi * 2 + b, h), jnp.logical_and(a == h, b == h),
            )

    gain_mate = take()
    send(gain, GM, gain_mate, mate)
    gain_in = pltpu.make_async_copy(gain, GO, rsem.at[take()])
    gain_in.start()

    def slot(yy, core):
        return E.at[yy % 2, (yy // 2) * 2 + core]

    def half(ref, i):
        return ref.at[pl.ds(i * 128, 128), :]

    e_p, e_m, e_op, e_om = take(2), take(2), take(), take()
    c_own, c_p, c_m, c_o = take(), take(2), take(2), take(2)
    for i in (0, 1):
        send(half(enc, i), half(slot(y, b), i), e_p + i, device(z, x, yp, b))
        send(half(enc, 1 - i), half(slot(y, b), 1 - i), e_m + 1 - i, device(z, x, ym, b))
    tok, tok_mate = take(), take()
    send(prev, T.at[a], tok, device(z, x, (yhi * 2 + b + 1) % NY, a))

    own = pltpu.make_async_copy(enc, slot(y, b), rsem.at[take()])
    own.start()
    send(enc, slot(y, b), c_own, mate)

    ax, az, bz, bx, bo = ([take(m) for _ in GROUPS] for m in (3, 8, 8, 16, 8))
    up, down = device(zp, x, y, b), device(zm, x, y, b)
    east, west = device(z, xp, y, b), device(z, xm, y, b)

    def zz(d):
        return (z + d + NZ) % NZ

    def pass_on(ref, i, to):
        send(ref, ref, i, to)

    def a_ring(g, step):
        ref, i = WA[g], az[g] + 2 * (step - 1)
        if step > 1:
            arrived(ref.at[zz(1 - step)], i - 2)
            arrived(ref.at[zz(step - 1)], i - 1)
        if step < 4:
            pass_on(ref.at[zz(1 - step)], i, up)
            pass_on(ref.at[zz(step - 1)], i + 1, down)
        else:
            pass_on(ref.at[zz(-3), pl.ds(0, 2)], i, up)
            pass_on(ref.at[zz(3), pl.ds(2, 2)], i + 1, down)

    def a_end(g):
        arrived(WA[g].at[zz(4), pl.ds(0, 2)], az[g] + 6)
        arrived(WA[g].at[zz(4), pl.ds(2, 2)], az[g] + 7)

    def b_ring(g, step):
        ref, i = WB[g].at[x], bz[g] + 2 * (step - 1)
        if step > 1:
            arrived(ref.at[zz(1 - step)], i - 2)
            arrived(ref.at[zz(step - 1)], i - 1)
        if step < 4:
            pass_on(ref.at[zz(1 - step)], i, up)
            pass_on(ref.at[zz(step - 1)], i + 1, down)
        else:
            pass_on(ref.at[zz(-3), :, pl.ds(0, 16), :], i, up)
            pass_on(ref.at[zz(3), :, pl.ds(16, 16), :], i + 1, down)

    def b_end(g):
        arrived(WB[g].at[x, zz(4), :, pl.ds(0, 16), :], bz[g] + 6)
        arrived(WB[g].at[x, zz(4), :, pl.ds(16, 16), :], bz[g] + 7)

    def b_out(g, *steps):
        for d in steps:
            block = WB[g].at[x, zz(d)]
            pass_on(block, bx[g] + 2 * (d % 8), east)
            pass_on(block, bx[g] + 2 * (d % 8) + 1, west)

    def b_on(g, *steps):
        for d in steps:
            arrived(WB[g].at[xm, zz(d)], bx[g] + 2 * (d % 8))
            arrived(WB[g].at[xp, zz(d)], bx[g] + 2 * (d % 8) + 1)
            if d <= 0:
                pass_on(WB[g].at[xm, zz(d)], bo[g] + d % 8, east)
            else:
                pass_on(WB[g].at[xp, zz(d)], bo[g] + d % 8, west)

    def b_far(g):
        for d in range(-3, 5):
            arrived(WB[g].at[xo, zz(d)], bo[g] + d % 8)

    def s1(g):
        used = sorted({w for units in GROUPS[g] for w, _ in units})
        for w in used:
            for i in (0, 1):
                arrived(S.at[names.index(w), i], quad[names.index(w)] + 2 * b + i)
        for path, units in enumerate(GROUPS[g]):
            for n, (w, u) in enumerate(units):
                unit = S[names.index(w), :, :, u * 128 : (u + 1) * 128].reshape(32, 128)
                if path == 0:
                    WA[g][z, x, n] = unit
                else:
                    WB[g][x, z, n] = unit
        b_ring(g, 1)
        for i, xi in enumerate((xp, xm, xo)):
            send(WA[g].at[z, x], WA[g].at[z, x], ax[g] + i, device(z, xi, y, b))
        b_out(g, 0)

    def s2(g):
        b_ring(g, 2)
        b_out(g, -1, 1)
        for i, xi in enumerate((xm, xp, xo)):
            arrived(WA[g].at[z, xi], ax[g] + i)
        a_ring(g, 1)

    def s3(g):
        b_ring(g, 3)
        b_out(g, -2, 2)
        b_on(g, 0)

    def s4(g):
        b_ring(g, 4)
        b_out(g, -3, 3)
        a_ring(g, 2)
        b_on(g, -1, 1)

    def s5(g):
        b_end(g)
        b_out(g, 4)
        b_on(g, -2, 2)

    def s6(g):
        a_ring(g, 3)
        b_on(g, -3, 3)

    def s7(g):
        a_ring(g, 4)
        b_on(g, 4)

    def s8(g):
        a_end(g)
        b_far(g)

    def e1():
        arrived(T.at[b], tok)
        send(T.at[b], T.at[b], tok_mate, mate)

    def e2():
        arrived(half(slot(ym, b), 0), e_p)
        send(half(slot(ym, b), 0), half(slot(ym, b), 0), e_op, device(z, x, yp, b))
        send(half(slot(ym, b), 0), half(slot(ym, b), 0), c_m, mate)
        arrived(half(slot(yp, b), 1), e_m + 1)
        send(half(slot(yp, b), 1), half(slot(yp, b), 1), e_om, device(z, x, ym, b))
        send(half(slot(yp, b), 1), half(slot(yp, b), 1), c_p + 1, mate)

    def e3():
        arrived(half(slot(ym, b), 1), e_p + 1)
        send(half(slot(ym, b), 1), half(slot(ym, b), 1), c_m + 1, mate)
        arrived(half(slot(yp, b), 0), e_m)
        send(half(slot(yp, b), 0), half(slot(yp, b), 0), c_p, mate)

    def e4():
        arrived(half(slot(yo, b), 0), e_op)
        send(half(slot(yo, b), 0), half(slot(yo, b), 0), c_o, mate)
        arrived(half(slot(yo, b), 1), e_om)
        send(half(slot(yo, b), 1), half(slot(yo, b), 1), c_o + 1, mate)

    def weight(w):
        units = []
        for u in range(4):
            for g, paths in enumerate(GROUPS):
                if (w, u) in paths[0]:
                    units.append(WA[g][:, :, paths[0].index((w, u))].reshape(D, 128))
                if (w, u) in paths[1]:
                    unit = WB[g][:, :, paths[1].index((w, u))]
                    units.append(jnp.swapaxes(unit, 0, 1).reshape(D, 128))
        return jnp.concatenate(units, axis=1)

    def cq():
        arrived(T.at[1 - b], tok_mate)
        arrived(GM, gain_mate)
        gain_in.wait()
        scale = jnp.where(a == b, GO[...], GM[...])
        normed = rms(T[...].reshape(2 * DEC, D).astype(F32), scale).astype(BF)
        Q[...] = dot(normed, weight("q")).astype(BF)

    def states(step):
        yy = (y + step) % NY
        return [
            (
                E[yy % 2, (yy // 2) * 2 + core],
                pl.ds(pl.multiple_of((yy % 2) * ENC + ((yy // 2) * 2 + core) * 256, 256), 256),
            )
            for core in (0, 1)
        ]

    def ready(step):
        if step == 0:
            own.wait()
            arrived(slot(y, 1 - b), c_own)
            return
        yy, sem = {1: (yp, c_p), 3: (ym, c_m), 2: (yo, c_o)}[step]
        for i in (0, 1):
            arrived(half(slot(yy, 1 - b), i), sem + i)

    def ck(step):
        ready(step)
        for block, rows in states(step):
            K[rows, :] = dot(block, weight("k")).astype(BF)

    def cv(step):
        for block, rows in states(step):
            V[rows, :] = dot(block, weight("v")).astype(BF)

    lane = lax.broadcasted_iota(jnp.int32, (DEC, 128), 1)

    def at(seq):
        @pl.loop(0, 4)
        def _(pair):
            columns = pl.ds(pl.multiple_of(pair * 128, 128), 128)
            rows = pl.ds(seq * DEC, DEC)
            keys = pl.ds(seq * ENC, ENC)
            q = Q[rows, columns]
            both = jnp.concatenate(
                [jnp.where(lane < 64, q, 0).astype(BF), jnp.where(lane >= 64, q, 0).astype(BF)],
                axis=0,
            )
            scores = lax.dot_general(
                both, K[keys, columns], (((1,), (1,)), ((), ())), preferred_element_type=F32
            )
            top = jnp.max(scores, axis=-1, keepdims=True)
            expo = jnp.exp((scores - top) * 0.125)
            probs = (expo * (1.0 / jnp.sum(expo, axis=-1, keepdims=True))).astype(BF)
            mixed2 = dot(probs, V[keys, columns])
            C[b, rows, columns] = jnp.where(lane < 64, mixed2[:DEC], mixed2[DEC:]).astype(BF)

    ops = dict(s1=s1, s2=s2, s3=s3, s4=s4, s5=s5, s6=s6, s7=s7, s8=s8, e1=e1, e2=e2, e3=e3, e4=e4,
               cq=cq, ck=ck, cv=cv, at=at, rd=ready)
    for op in plan:
        name, _, arg = op.partition(" ")
        ops[name](*([int(arg)] if arg else []))

    ctx = take()
    send(C.at[b], C.at[b], ctx, mate)
    arrived(C.at[1 - b], ctx)
    wout = weight("o")
    attn = dot(C[0], wout[:HALF]) + dot(C[1], wout[HALF:])
    mine = pl.ds(pl.multiple_of(b * HALF, HALF), HALF)
    for c in (0, 1):
        MX[c] = (T[c, :, mine].astype(F32) + attn[c * DEC : (c + 1) * DEC]).astype(BF)

    home = take(4)
    for c in (0, 1):
        src, dst = MX.at[c], H.at[b]
        i = home + 2 * c + b
        here = jnp.logical_and(a == c, b == c)
        to = device(z, x, yhi * 2 + c, a)
        send_or_keep(src, dst, i, to, here)
    for h in (0, 1):
        arrived(H.at[h], home + 2 * a + h)
    for h in (0, 1):
        out[:, h * HALF : (h + 1) * HALF] = H[h]
    for wait in pending:
        wait()


def attention(prev, enc, wq, wk, wv, wo, gain):
    vmem = pl.BlockSpec(memory_space=pltpu.VMEM)
    return pl.pallas_call(
        functools.partial(attention_kernel, PLAN),
        name="attention",
        out_shape=jax.ShapeDtypeStruct((DEC, D), BF),
        in_specs=[pl.BlockSpec(memory_space=pl.ANY)] * 7,
        out_specs=vmem,
        scratch_shapes=[
            pltpu.VMEM((2, 4, 256, D), BF),
            pltpu.VMEM((NZ, NX, len(GROUPS[0][0]), 32, 128), BF),
            pltpu.VMEM((NX, NZ, len(GROUPS[0][1]), 32, 128), BF),
            pltpu.VMEM((NZ, NX, len(GROUPS[1][0]), 32, 128), BF),
            pltpu.VMEM((NX, NZ, len(GROUPS[1][1]), 32, 128), BF),
            pltpu.VMEM((2, DEC, D), BF),
            pltpu.VMEM((2 * ENC, HALF), BF),
            pltpu.VMEM((2 * ENC, HALF), BF),
            pltpu.VMEM((2 * DEC, HALF), BF),
            pltpu.VMEM((2, 2 * DEC, HALF), BF),
            pltpu.VMEM((2, DEC, HALF), BF),
            pltpu.VMEM((2, DEC, HALF), BF),
            pltpu.VMEM((1, D), F32),
            pltpu.VMEM((1, D), F32),
            pltpu.VMEM((4, 2, 16, HALF), BF),
            pltpu.SemaphoreType.DMA((SEMS_A,)),
            pltpu.SemaphoreType.DMA((SEMS_A,)),
        ],
        compiler_params=pltpu.CompilerParams(
            collective_id=1, has_side_effects=True, vmem_limit_bytes=48 << 20
        ),
    )(prev, enc, wq, wk, wv, wo, gain)


CHUNKS = ((1, 5), (3, 7), (2, 6), (0, 4))


def moe_kernel(mixed, gain, routes, routes_t, gates, spread, gather, wg, wu, wd, out,
               G, U, DN, B0, BUF, X, XR, HID, OWN, PS, PX, RB, R, RR,
               wsem, dsend, drecv, fsend, frecv, psend, precv, rsend, rrecv):
    z, x, y, b = place_of()
    sec, exp = lax.axis_index("section"), lax.axis_index("expert")
    here, a = exp // 2, exp % 2
    partner = (sec, exp + 1 - 2 * a)

    loads = [
        pltpu.make_async_copy(src, dst, wsem.at[i])
        for i, (src, dst) in enumerate(((wg, G), (wu, U), (wd, DN)))
    ]
    for load in loads:
        load.start()

    def zt(zk, sign):
        return (z + sign * zk + NZ) % NZ

    def xt(xk, sign):
        return (x + sign * xk + NX) % NX

    def plane(zi, xi):
        return (sec, (zi * NX + xi) * 2 + a)

    bar = pltpu.get_barrier_semaphore()

    @pl.loop(1, 32)
    def _(k):
        pl.semaphore_signal(
            bar, inc=1, device_id=plane(zt(k // NX, -1), xt(k % NX, -1)), device_id_type=MESH
        )

    pl.semaphore_signal(bar, inc=1, device_id=partner, device_id_type=MESH)

    def remote(src, dst, s, r, to):
        return pltpu.make_async_remote_copy(
            src_ref=src, dst_ref=dst, send_sem=s, recv_sem=r, device_id=to, device_id_type=MESH
        )

    def to_blocks(rows):
        stacked = jnp.concatenate([rows[:, q * QUART : (q + 1) * QUART] for q in range(4)], axis=0)
        return dot(spread[...], stacked).astype(BF).reshape(4, 48, QUART)

    def to_rows(blocks, dst, first):
        stacked = dot(gather[...], blocks.reshape(192, QUART)).astype(BF)
        for q in range(4):
            dst[pl.ds(first, 48), q * QUART : (q + 1) * QUART] = stacked[q * 48 : (q + 1) * 48]

    moe_in = rms(mixed[...].astype(F32), gain[...]).astype(BF)
    expert_r = lax.broadcasted_iota(jnp.int32, (EXPERTS, DEC), 0)
    hot = [(expert_r == routes_t[k : k + 1, :]).astype(F32) for k in (0, 1)]
    t0 = lax.broadcasted_iota(jnp.int32, (DEC, DEC), 0)
    t1 = lax.broadcasted_iota(jnp.int32, (DEC, DEC), 1)
    count = dot((hot[0] + hot[1]).astype(BF), (t0 < t1).astype(BF))
    slot_id = lax.broadcasted_iota(jnp.int32, (SLOTS, DEC), 0)
    place = jnp.zeros((SLOTS, DEC), F32)
    for k in (0, 1):
        slot = jnp.sum(count * hot[k], axis=0, keepdims=True).astype(jnp.int32)
        position = routes_t[k : k + 1, :] * CAP + slot
        place = place + (slot_id == position).astype(F32)
    B0[...] = dot(place.astype(BF), moe_in).astype(BF)
    pl.semaphore_wait(bar, 32)

    def rows_of(zi):
        return pl.ds(pl.multiple_of(zi * 48, 16), 48)

    def exchange(zi, first, zk, src, dst, s, r, sign):
        @pl.loop(first, NX)
        def _(xk):
            xi = xt(xk, sign)
            k = zk * NX + xk
            remote(src.at[zi * NX + xi], dst.at[here], s.at[k], r.at[k], plane(zi, xi)).start()

    for chunk in CHUNKS:
        for zk in chunk:
            zi = zt(zk, 1)
            BUF[pl.ds(zi * NX, NX)] = to_blocks(B0[rows_of(zi), :])
            exchange(zi, int(zk == 0), zk, BUF, X.at[0], dsend, drecv, 1)
    X[0, here] = BUF[here]

    def group(ref, zk):
        return ref.at[pl.ds(zt(zk, -1) * NX, NX)]

    def forward(chunk):
        for zk in chunk:
            zi = zt(zk, -1)

            @pl.loop(int(zk == 0), NX)
            def _(xk):
                src = X.at[0, zi * NX + xt(xk, -1)]
                remote(src, src, dsend.at[zk * NX + xk], drecv.at[zk * NX + xk], partner).wait_recv()

            remote(group(X.at[0], zk), group(X.at[1], zk), fsend.at[zk], frecv.at[zk], partner).start()

    def swap(j):
        return remote(PS.at[j], PX.at[j], psend.at[j], precv.at[j], partner)

    def work(j, chunk):
        for i, zk in enumerate(chunk):
            remote(group(X.at[1], zk), group(X.at[1], zk), fsend.at[zk], frecv.at[zk], partner).wait_recv()
            to_rows(group(X.at[0], zk)[...], XR, i * 48)
            to_rows(group(X.at[1], zk)[...], XR, 96 + i * 48)
        if j == 0:
            for load in loads:
                load.wait()
        rows = XR[...]
        gated, upper = dot(rows, G[...]), dot(rows, U[...])
        HID[...] = (jax.nn.gelu(gated) * upper).astype(BF)
        PS[j] = dot(HID[96:, :], DN[...]).astype(BF)
        swap(j).start()
        OWN[j] = dot(HID[:96, :], DN[...])

    def back(j, chunk):
        swap(j).wait()
        total = (OWN[j] + PX[j].astype(F32)).astype(BF)
        for i, zk in enumerate(chunk):
            zi = zt(zk, -1)
            RB[pl.ds(zi * NX, NX)] = to_blocks(total[i * 48 : (i + 1) * 48])
            exchange(zi, int(zk == 0), zk, RB, R, rsend, rrecv, -1)
            if zk == 0:
                R[here] = RB[here]

    for j in range(len(CHUNKS) + 2):
        if j < len(CHUNKS):
            forward(CHUNKS[j])
        if 1 <= j <= len(CHUNKS):
            work(j - 1, CHUNKS[j - 1])
        if j >= 2:
            back(j - 2, CHUNKS[j - 2])

    expert_c = lax.broadcasted_iota(jnp.int32, (DEC, EXPERTS), 1)
    hot = [(expert_c == routes[:, k : k + 1]).astype(F32) for k in (0, 1)]
    count = dot((t1 < t0).astype(BF), (hot[0] + hot[1]).astype(BF))
    slot_id = lax.broadcasted_iota(jnp.int32, (DEC, SLOTS), 1)
    picks = []
    for k in (0, 1):
        slot = jnp.sum(count * hot[k], axis=1, keepdims=True).astype(jnp.int32)
        picks.append((slot_id == routes[:, k : k + 1] * CAP + slot).astype(F32).astype(BF))

    for chunk in CHUNKS:
        for zk in chunk:
            zi = zt(zk, 1)
            remote(group(X.at[0], zk), group(X.at[0], zk), fsend.at[zk], frecv.at[zk], partner).wait_send()

            @pl.loop(int(zk == 0), NX)
            def _(xk):
                k = zk * NX + xk
                block = R.at[zi * NX + xt(xk, 1)]
                remote(block, block, rsend.at[k], rrecv.at[k], partner).wait()
                remote(block, block, dsend.at[k], drecv.at[k], partner).wait_send()

            to_rows(R[pl.ds(zi * NX, NX)], RR, pl.multiple_of(zi * 48, 16))
    total = mixed[...].astype(F32)
    moe = [dot(picks[k], RR[...]) * gates[:, k : k + 1] for k in (0, 1)]
    out[...] = (total + (moe[0] + moe[1])).astype(BF)


def spread_matrix():
    m = np.zeros((192, 192), np.float32)
    for s in range(4):
        for q in range(4):
            for c in range(CAP):
                m[s * 48 + q * 12 + c, q * 48 + s * 12 + c] = 1
    return m


def experts(mixed, gain, routes, gates, wg, wu, wd):
    vmem, hbm = pl.BlockSpec(memory_space=pltpu.VMEM), pl.BlockSpec(memory_space=pl.ANY)
    spread = spread_matrix()
    dma = pltpu.SemaphoreType.DMA
    return pl.pallas_call(
        moe_kernel,
        name="experts",
        out_shape=jax.ShapeDtypeStruct((DEC, D), BF),
        in_specs=[vmem] * 7 + [hbm] * 3,
        out_specs=vmem,
        scratch_shapes=[
            pltpu.VMEM((D, PIECE), BF),
            pltpu.VMEM((D, PIECE), BF),
            pltpu.VMEM((PIECE, D), BF),
            pltpu.VMEM((SLOTS, D), BF),
            pltpu.VMEM((32, 48, QUART), BF),
            pltpu.VMEM((2, 32, 48, QUART), BF),
            pltpu.VMEM((192, D), BF),
            pltpu.VMEM((192, PIECE), BF),
            pltpu.VMEM((4, 96, D), F32),
            pltpu.VMEM((4, 96, D), BF),
            pltpu.VMEM((4, 96, D), BF),
            pltpu.VMEM((32, 48, QUART), BF),
            pltpu.VMEM((32, 48, QUART), BF),
            pltpu.VMEM((SLOTS, D), BF),
            dma((3,)),
            dma((32,)),
            dma((32,)),
            dma((8,)),
            dma((8,)),
            dma((4,)),
            dma((4,)),
            dma((32,)),
            dma((32,)),
        ],
        compiler_params=pltpu.CompilerParams(
            collective_id=2, has_side_effects=True, vmem_limit_bytes=56 << 20
        ),
    )(mixed, gain, routes, routes.T, gates, jnp.asarray(spread, BF), jnp.asarray(spread.T, BF), wg, wu, wd)


def per_device(previous, encoder_states, routes, gate_values, gain_attn, gain_moe, query_weight,
               key_weight, value_weight, out_weight, expert_gate, expert_up, expert_down):
    mixed = attention(
        previous[0, 0], encoder_states[0], query_weight[0], key_weight[0], value_weight[0],
        out_weight[0], gain_attn,
    )
    result = experts(
        mixed, gain_moe, routes[0, 0], gate_values[0, 0], expert_gate[0, 0], expert_up[0, 0],
        expert_down[0, 0],
    )
    return result.reshape(previous.shape)


def solution(mesh):
    in_specs = (
        P("section", "expert", None, None),
        P("expert", "section", None),
        P("section", "expert", None, None),
        P("section", "expert", None, None),
        P("section", None),
        P("section", None),
        P("section", "expert", None),
        P("section", "expert", None),
        P("section", "expert", None),
        P("section", "expert", None),
        P("section", "expert", None, None),
        P("section", "expert", None, None),
        P("section", "expert", None, None),
    )
    out_specs = P("section", "expert", None, None)
    return jax.shard_map(
        per_device, mesh=mesh, in_specs=in_specs, out_specs=out_specs, check_vma=False
    )
```

time: 174 us -> 138 us (0.79)
  the two profiles are of different devices: /device:TPU:64 before, /device:TPU:16 now
where the time goes in v2:
time: 138 us; the launch traced here: 136 us
  Pallas kernels  125 us (91%)
  local copies, waits for them, and re-layouts  10.9 us (8%)
    pallas_call x1, Pallas kernels, attention(): pl.pallas_call(functools.partial(attention_kernel, PLAN), name='attention...  63.7 us
    pallas_call x1, Pallas kernels, experts(): pl.pallas_call(moe_kernel, name='experts', out_shape=jax.ShapeDtypeStruct...  61.5 us
    unnamed x18, local copies, waits for them, and re-layouts  9.47 us

profile of v2, /device:TPU:16, one launch (start us, length us, event | category | flops | bytes accessed | tf_op | source)
XLA Modules:
  0.0 136.1 jit_solution(6741305302346387153)
XLA Ops:
  0.0 1.4 %copy.16 = f32[1,1,128,2]{3,2,1,0:T(8,128)} copy(f32[1,1,128,2]{2,3,1,0:T(2,128)} %param.18) | data formatting | bytes 2048 | tf_op args[3]
  1.4 1.4 %copy.17.routes = s32[128,2]{1,0:T(8,128)} copy(s32[128,2]{0,1:T(2,128)} %bitcast.25) | data formatting | bytes 2048 | tf_op jit(solution)/shard_map/squeeze | solution.py:665
  2.8 0.0 copy-start.1
  2.8 1.0 copy-done.1
  3.8 0.0 copy-start.2
  3.8 0.9 copy-done.2
  4.8 0.0 copy-start.3
  4.8 0.8 copy-done.3
  5.6 0.0 copy-start.4
  5.6 0.8 copy-done.4
  6.3 0.0 copy-start.5
  6.3 0.8 copy-done.5
  7.1 0.0 copy-start.6
  7.1 0.8 copy-done.6
  7.8 0.0 copy-start.7
  7.8 0.7 copy-done.7
  8.5 63.7 %attention.1.mixed = bf16[128,1024]{1,0:T(8,128)(2,1)S(1)} custom-call(bf16[128,1024]{1,0:T(8,128)(2,1)S(1)} %bitcast.15, bf16[256,1024]{1,0:T(8,128)(2,1)S(1)} %bitcast.14, bf16[16,1024]{1,0:T(8,128)(2,1)S(1)} %bitcast.16, bf16[16,1024]{1,0:T(8,128)(2,1)S(1)} %bitcast.17, bf16[16,1024]{1,0:T(8,128)(2,1)S(1)} %bitcast.18, bf16[16,1024]{1,0:T(8,128)(2,1)S(1)} %bitcast.19, ...), custom_call_target="tpu_custom_call" | custom-call | tf_op jit(solution)/shard_map/attention/pallas_call | solution.py:417
  72.2 0.0 copy-start
  72.2 0.7 copy-done
  72.9 61.5 %experts.1 = bf16[128,1024]{1,0:T(8,128)(2,1)} custom-call(bf16[128,1024]{1,0:T(8,128)(2,1)} %copy-done, f32[1,1024]{1,0:T(1,128)} %gain.3, s32[128,2]{1,0:T(8,128)} %copy.17.routes, s32[2,128]{1,0:T(2,128)} %bitcast.26, f32[128,2]{1,0:T(8,128)} %bitcast.24, bf16[192,192]{1,0:T(8,128)(2,1)} %constant.2.clone.spread.gather, ...), custom_call_target="tpu_custom_call" | custom-call | tf_op jit(solution)/shard_map/experts/pallas_call | solution.py:621
  134.4 1.7 %copy.19 = bf16[1,1,128,1024]{3,2,1,0:T(8,128)(2,1)} copy(bf16[1,1,128,1024]{3,2,1,0:T(8,128)(2,1)} %bitcast.23) | data formatting | bytes 524288
Async XLA Ops:
  2.8 1.0 copy-start.1
  3.8 0.9 copy-start.2
  4.8 0.8 copy-start.3
  5.6 0.8 copy-start.4
  6.3 0.8 copy-start.5
  7.1 0.8 copy-start.6
  7.8 0.7 copy-start.7
  72.2 0.7 copy-start

commit v3 on v2

--- a/solution.py
+++ b/solution.py
@@ -2,7 +2,6 @@
 
 import jax
 import jax.numpy as jnp
-import numpy as np
 from jax import lax
 from jax.experimental import pallas as pl
 from jax.experimental.pallas import tpu as pltpu
@@ -77,13 +76,15 @@
         5: ["e2"],
         7: ["e3", "e1"],
         8: ["e4", "ck 0", "ck 1"],
-        9: ["ck 3", "ck 2", "cv 0", "cv 1", "cv 3", "cv 2", "cq", "at 0"],
-        10: ["at 1"],
+        6: ["ld"],
+        9: ["ck 3", "ck 2", "cv 0", "cv 1", "cv 3", "cv 2", "cq", "at 0", "cx 0"],
+        10: ["at 1", "cx 1", "op 0", "op 1", "hm"],
     },
 )
 
 
-def attention_kernel(plan, prev, enc, wq, wk, wv, wo, gain, out, E, WA0, WB0, WA1, WB1, T, K, V, Q, C, MX, H, GM, GO, S, ssem, rsem):
+def attention_part(plan, prev, enc, wq, wk, wv, wo, gain, E, WA0, WB0, WA1, WB1, T, K, V, Q, C, MX, H,
+                   GM, GO, S, ssem, rsem, load):
     WA, WB = (WA0, WA1), (WB0, WB1)
     z, x, y, b = place_of()
     a, yhi = y % 2, y // 2
@@ -111,7 +112,13 @@
     ]
     for other in greet:
         pl.semaphore_signal(bar, inc=1, device_id=other, device_id_type=MESH)
-    pl.semaphore_wait(bar, len(greet))
+
+    @pl.loop(1, 32)
+    def _(k):
+        zi, xi = (z + k // NX) % NZ, (x + k % NX) % NX
+        pl.semaphore_signal(bar, inc=1, device_id=device(zi, xi, y, b), device_id_type=MESH)
+
+    pl.semaphore_wait(bar, len(greet) + 31)
 
     def remote(src, dst, i, to):
         return pltpu.make_async_remote_copy(
@@ -382,43 +389,216 @@
             mixed2 = dot(probs, V[keys, columns])
             C[b, rows, columns] = jnp.where(lane < 64, mixed2[:DEC], mixed2[DEC:]).astype(BF)
 
+    ctx, home = take(2), take(4)
+    mine = pl.ds(pl.multiple_of(b * HALF, HALF), HALF)
+
+    def cx(seq):
+        own_half = C.at[b, pl.ds(seq * DEC, DEC), :]
+        send(own_half, own_half, ctx + seq, mate)
+
+    def op(seq):
+        rows = pl.ds(seq * DEC, DEC)
+        arrived(C.at[1 - b, rows, :], ctx + seq)
+        wout = weight("o")
+        attn = dot(C[0, rows, :], wout[:HALF]) + dot(C[1, rows, :], wout[HALF:])
+        MX[seq] = (T[seq, :, mine].astype(F32) + attn).astype(BF)
+        send_or_keep(
+            MX.at[seq], H.at[b], home + 2 * seq + b, device(z, x, yhi * 2 + seq, a),
+            jnp.logical_and(a == seq, b == seq),
+        )
+
+    def hm():
+        for h in (0, 1):
+            arrived(H.at[h], home + 2 * a + h)
+
     ops = dict(s1=s1, s2=s2, s3=s3, s4=s4, s5=s5, s6=s6, s7=s7, s8=s8, e1=e1, e2=e2, e3=e3, e4=e4,
-               cq=cq, ck=ck, cv=cv, at=at, rd=ready)
-    for op in plan:
-        name, _, arg = op.partition(" ")
+               cq=cq, ck=ck, cv=cv, at=at, cx=cx, op=op, hm=hm, ld=load)
+    for step in plan:
+        name, _, arg = step.partition(" ")
         ops[name](*([int(arg)] if arg else []))
 
-    ctx = take()
-    send(C.at[b], C.at[b], ctx, mate)
-    arrived(C.at[1 - b], ctx)
-    wout = weight("o")
-    attn = dot(C[0], wout[:HALF]) + dot(C[1], wout[HALF:])
-    mine = pl.ds(pl.multiple_of(b * HALF, HALF), HALF)
-    for c in (0, 1):
-        MX[c] = (T[c, :, mine].astype(F32) + attn[c * DEC : (c + 1) * DEC]).astype(BF)
-
-    home = take(4)
-    for c in (0, 1):
-        src, dst = MX.at[c], H.at[b]
-        i = home + 2 * c + b
-        here = jnp.logical_and(a == c, b == c)
-        to = device(z, x, yhi * 2 + c, a)
-        send_or_keep(src, dst, i, to, here)
-    for h in (0, 1):
-        arrived(H.at[h], home + 2 * a + h)
-    for h in (0, 1):
-        out[:, h * HALF : (h + 1) * HALF] = H[h]
+    return pending
+
+
+CHUNKS = ((1, 5), (3, 7), (2, 6), (0, 4))
+
+
+def experts_part(mixed, gain, routes_t, gates_t, loads, out,
+                 G, U, DN, B0, BUF, X, XR, HID, OWN, PS, PX, RB, R, RR, PK, SP,
+                 dsend, drecv, fsend, frecv, psend, precv, rsend, rrecv):
+    z, x, y, b = place_of()
+    sec, exp = lax.axis_index("section"), lax.axis_index("expert")
+    here, a = exp // 2, exp % 2
+    partner = (sec, exp + 1 - 2 * a)
+
+    def zt(zk, sign):
+        return (z + sign * zk + NZ) % NZ
+
+    def xt(xk, sign):
+        return (x + sign * xk + NX) % NX
+
+    def plane(zi, xi):
+        return (sec, (zi * NX + xi) * 2 + a)
+
+    def remote(src, dst, s, r, to):
+        return pltpu.make_async_remote_copy(
+            src_ref=src, dst_ref=dst, send_sem=s, recv_sem=r, device_id=to, device_id_type=MESH
+        )
+
+    def to_blocks(rows):
+        stacked = jnp.concatenate([rows[:, q * QUART : (q + 1) * QUART] for q in range(4)], axis=0)
+        return dot(SP[...], stacked).astype(BF).reshape(4, 48, QUART)
+
+    def to_rows(blocks, dst, first):
+        stacked = dot(SP[...], blocks.reshape(192, QUART)).astype(BF)
+        for q in range(4):
+            dst[pl.ds(first, 48), q * QUART : (q + 1) * QUART] = stacked[q * 48 : (q + 1) * 48]
+
+    moe_in = rms(mixed.astype(F32), gain[...]).astype(BF)
+    expert_r = lax.broadcasted_iota(jnp.int32, (EXPERTS, DEC), 0)
+    hot = [(expert_r == routes_t[k : k + 1, :]).astype(F32) for k in (0, 1)]
+    t0 = lax.broadcasted_iota(jnp.int32, (DEC, DEC), 0)
+    t1 = lax.broadcasted_iota(jnp.int32, (DEC, DEC), 1)
+    count = dot((hot[0] + hot[1]).astype(BF), (t0 < t1).astype(BF))
+    slot_id = lax.broadcasted_iota(jnp.int32, (SLOTS, DEC), 0)
+    for k in (0, 1):
+        slot = jnp.sum(count * hot[k], axis=0, keepdims=True).astype(jnp.int32)
+        position = routes_t[k : k + 1, :] * CAP + slot
+        PK[k] = (slot_id == position).astype(F32).astype(BF)
+    place = PK[0] + PK[1]
+    B0[...] = dot(place, moe_in).astype(BF)
+
+    def rows_of(zi):
+        return pl.ds(pl.multiple_of(zi * 48, 16), 48)
+
+    def exchange(zi, first, zk, src, dst, s, r, sign):
+        @pl.loop(first, NX)
+        def _(xk):
+            xi = xt(xk, sign)
+            k = zk * NX + xk
+            remote(src.at[zi * NX + xi], dst.at[here], s.at[k], r.at[k], plane(zi, xi)).start()
+
+    for chunk in CHUNKS:
+        for zk in chunk:
+            zi = zt(zk, 1)
+            BUF[pl.ds(zi * NX, NX)] = to_blocks(B0[rows_of(zi), :])
+            exchange(zi, int(zk == 0), zk, BUF, X.at[0], dsend, drecv, 1)
+    X[0, here] = BUF[here]
+
+    def group(ref, zk):
+        return ref.at[pl.ds(zt(zk, -1) * NX, NX)]
+
+    def forward(chunk):
+        for zk in chunk:
+            zi = zt(zk, -1)
+
+            @pl.loop(int(zk == 0), NX)
+            def _(xk):
+                src = X.at[0, zi * NX + xt(xk, -1)]
+                remote(src, src, dsend.at[zk * NX + xk], drecv.at[zk * NX + xk], partner).wait_recv()
+
+            remote(group(X.at[0], zk), group(X.at[1], zk), fsend.at[zk], frecv.at[zk], partner).start()
+
+    def swap(j):
+        return remote(PS.at[j], PX.at[j], psend.at[j], precv.at[j], partner)
+
+    def work(j, chunk):
+        for i, zk in enumerate(chunk):
+            remote(group(X.at[1], zk), group(X.at[1], zk), fsend.at[zk], frecv.at[zk], partner).wait_recv()
+            to_rows(group(X.at[0], zk)[...], XR, i * 48)
+            to_rows(group(X.at[1], zk)[...], XR, 96 + i * 48)
+        if j == 0:
+            for load in loads:
+                load.wait()
+        rows = XR[...]
+        gated, upper = dot(rows, G[...]), dot(rows, U[...])
+        HID[...] = (jax.nn.gelu(gated) * upper).astype(BF)
+        PS[j] = dot(HID[96:, :], DN[...]).astype(BF)
+        swap(j).start()
+        OWN[j] = dot(HID[:96, :], DN[...])
+
+    def back(j, chunk):
+        swap(j).wait()
+        total = (OWN[j] + PX[j].astype(F32)).astype(BF)
+        for i, zk in enumerate(chunk):
+            zi = zt(zk, -1)
+            RB[pl.ds(zi * NX, NX)] = to_blocks(total[i * 48 : (i + 1) * 48])
+            exchange(zi, int(zk == 0), zk, RB, R, rsend, rrecv, -1)
+            if zk == 0:
+                R[here] = RB[here]
+
+    for j in range(len(CHUNKS) + 2):
+        if j < len(CHUNKS):
+            forward(CHUNKS[j])
+        if 1 <= j <= len(CHUNKS):
+            work(j - 1, CHUNKS[j - 1])
+        if j >= 2:
+            back(j - 2, CHUNKS[j - 2])
+
+    weights = [
+        jnp.transpose(jnp.broadcast_to(gates_t[k : k + 1, :], (DEC, DEC)))[:, :1] for k in (0, 1)
+    ]
+
+    for chunk in CHUNKS:
+        for zk in chunk:
+            zi = zt(zk, 1)
+            remote(group(X.at[0], zk), group(X.at[0], zk), fsend.at[zk], frecv.at[zk], partner).wait_send()
+
+            @pl.loop(int(zk == 0), NX)
+            def _(xk):
+                k = zk * NX + xk
+                block = R.at[zi * NX + xt(xk, 1)]
+                remote(block, block, rsend.at[k], rrecv.at[k], partner).wait()
+                remote(block, block, dsend.at[k], drecv.at[k], partner).wait_send()
+
+            to_rows(R[pl.ds(zi * NX, NX)], RR, pl.multiple_of(zi * 48, 16))
+    moe = [
+        lax.dot_general(PK[k], RR[...], (((0,), (0,)), ((), ())), preferred_element_type=F32)
+        * weights[k]
+        for k in (0, 1)
+    ]
+    out[...] = (mixed.astype(F32) + (moe[0] + moe[1])).astype(BF)
+
+
+def swap_matrix():
+    row = lax.broadcasted_iota(jnp.int32, (192, 192), 0)
+    column = lax.broadcasted_iota(jnp.int32, (192, 192), 1)
+    part = lax.shift_right_logical(row * 171, 11)
+    other = (part & 3) * 4 + lax.shift_right_logical(part, 2)
+    return (column == other * CAP + (row - part * CAP)).astype(F32).astype(BF)
+
+
+def relay_kernel(prev, enc, wq, wk, wv, wo, gain_attn, gain_moe, routes_t, gates_t,
+                 wg, wu, wd, out, *scratch):
+    first, second, wsem = scratch[:17], scratch[17:-1], scratch[-1]
+    H = first[11]
+    loads = [
+        pltpu.make_async_copy(src, dst, wsem.at[i])
+        for i, (src, dst) in enumerate(zip((wg, wu, wd), second[:3]))
+    ]
+
+    def load():
+        second[15][...] = swap_matrix()
+        for copy in loads:
+            copy.start()
+
+    pending = attention_part(
+        PLAN, prev, enc, wq, wk, wv, wo, gain_attn, *first, load
+    )
+    mixed = jnp.concatenate([H[0], H[1]], axis=1)
+    experts_part(mixed, gain_moe, routes_t, gates_t, loads, out, *second)
     for wait in pending:
         wait()
 
 
-def attention(prev, enc, wq, wk, wv, wo, gain):
-    vmem = pl.BlockSpec(memory_space=pltpu.VMEM)
+def relay(prev, enc, wq, wk, wv, wo, gain_attn, gain_moe, routes, gates, wg, wu, wd):
+    vmem, hbm = pl.BlockSpec(memory_space=pltpu.VMEM), pl.BlockSpec(memory_space=pltpu.HBM)
+    dma = pltpu.SemaphoreType.DMA
     return pl.pallas_call(
-        functools.partial(attention_kernel, PLAN),
-        name="attention",
+        relay_kernel,
+        name="relay",
         out_shape=jax.ShapeDtypeStruct((DEC, D), BF),
-        in_specs=[pl.BlockSpec(memory_space=pl.ANY)] * 7,
+        in_specs=[hbm] * 7 + [vmem] * 3 + [hbm] * 3,
         out_specs=vmem,
         scratch_shapes=[
             pltpu.VMEM((2, 4, 256, D), BF),
@@ -436,195 +616,8 @@
             pltpu.VMEM((1, D), F32),
             pltpu.VMEM((1, D), F32),
             pltpu.VMEM((4, 2, 16, HALF), BF),
-            pltpu.SemaphoreType.DMA((SEMS_A,)),
-            pltpu.SemaphoreType.DMA((SEMS_A,)),
-        ],
-        compiler_params=pltpu.CompilerParams(
-            collective_id=1, has_side_effects=True, vmem_limit_bytes=48 << 20
-        ),
-    )(prev, enc, wq, wk, wv, wo, gain)
-
-
-CHUNKS = ((1, 5), (3, 7), (2, 6), (0, 4))
-
-
-def moe_kernel(mixed, gain, routes, routes_t, gates, spread, gather, wg, wu, wd, out,
-               G, U, DN, B0, BUF, X, XR, HID, OWN, PS, PX, RB, R, RR,
-               wsem, dsend, drecv, fsend, frecv, psend, precv, rsend, rrecv):
-    z, x, y, b = place_of()
-    sec, exp = lax.axis_index("section"), lax.axis_index("expert")
-    here, a = exp // 2, exp % 2
-    partner = (sec, exp + 1 - 2 * a)
-
-    loads = [
-        pltpu.make_async_copy(src, dst, wsem.at[i])
-        for i, (src, dst) in enumerate(((wg, G), (wu, U), (wd, DN)))
-    ]
-    for load in loads:
-        load.start()
-
-    def zt(zk, sign):
-        return (z + sign * zk + NZ) % NZ
-
-    def xt(xk, sign):
-        return (x + sign * xk + NX) % NX
-
-    def plane(zi, xi):
-        return (sec, (zi * NX + xi) * 2 + a)
-
-    bar = pltpu.get_barrier_semaphore()
-
-    @pl.loop(1, 32)
-    def _(k):
-        pl.semaphore_signal(
-            bar, inc=1, device_id=plane(zt(k // NX, -1), xt(k % NX, -1)), device_id_type=MESH
-        )
-
-    pl.semaphore_signal(bar, inc=1, device_id=partner, device_id_type=MESH)
-
-    def remote(src, dst, s, r, to):
-        return pltpu.make_async_remote_copy(
-            src_ref=src, dst_ref=dst, send_sem=s, recv_sem=r, device_id=to, device_id_type=MESH
-        )
-
-    def to_blocks(rows):
-        stacked = jnp.concatenate([rows[:, q * QUART : (q + 1) * QUART] for q in range(4)], axis=0)
-        return dot(spread[...], stacked).astype(BF).reshape(4, 48, QUART)
-
-    def to_rows(blocks, dst, first):
-        stacked = dot(gather[...], blocks.reshape(192, QUART)).astype(BF)
-        for q in range(4):
-            dst[pl.ds(first, 48), q * QUART : (q + 1) * QUART] = stacked[q * 48 : (q + 1) * 48]
-
-    moe_in = rms(mixed[...].astype(F32), gain[...]).astype(BF)
-    expert_r = lax.broadcasted_iota(jnp.int32, (EXPERTS, DEC), 0)
-    hot = [(expert_r == routes_t[k : k + 1, :]).astype(F32) for k in (0, 1)]
-    t0 = lax.broadcasted_iota(jnp.int32, (DEC, DEC), 0)
-    t1 = lax.broadcasted_iota(jnp.int32, (DEC, DEC), 1)
-    count = dot((hot[0] + hot[1]).astype(BF), (t0 < t1).astype(BF))
-    slot_id = lax.broadcasted_iota(jnp.int32, (SLOTS, DEC), 0)
-    place = jnp.zeros((SLOTS, DEC), F32)
-    for k in (0, 1):
-        slot = jnp.sum(count * hot[k], axis=0, keepdims=True).astype(jnp.int32)
-        position = routes_t[k : k + 1, :] * CAP + slot
-        place = place + (slot_id == position).astype(F32)
-    B0[...] = dot(place.astype(BF), moe_in).astype(BF)
-    pl.semaphore_wait(bar, 32)
-
-    def rows_of(zi):
-        return pl.ds(pl.multiple_of(zi * 48, 16), 48)
-
-    def exchange(zi, first, zk, src, dst, s, r, sign):
-        @pl.loop(first, NX)
-        def _(xk):
-            xi = xt(xk, sign)
-            k = zk * NX + xk
-            remote(src.at[zi * NX + xi], dst.at[here], s.at[k], r.at[k], plane(zi, xi)).start()
-
-    for chunk in CHUNKS:
-        for zk in chunk:
-            zi = zt(zk, 1)
-            BUF[pl.ds(zi * NX, NX)] = to_blocks(B0[rows_of(zi), :])
-            exchange(zi, int(zk == 0), zk, BUF, X.at[0], dsend, drecv, 1)
-    X[0, here] = BUF[here]
-
-    def group(ref, zk):
-        return ref.at[pl.ds(zt(zk, -1) * NX, NX)]
-
-    def forward(chunk):
-        for zk in chunk:
-            zi = zt(zk, -1)
-
-            @pl.loop(int(zk == 0), NX)
-            def _(xk):
-                src = X.at[0, zi * NX + xt(xk, -1)]
-                remote(src, src, dsend.at[zk * NX + xk], drecv.at[zk * NX + xk], partner).wait_recv()
-
-            remote(group(X.at[0], zk), group(X.at[1], zk), fsend.at[zk], frecv.at[zk], partner).start()
-
-    def swap(j):
-        return remote(PS.at[j], PX.at[j], psend.at[j], precv.at[j], partner)
-
-    def work(j, chunk):
-        for i, zk in enumerate(chunk):
-            remote(group(X.at[1], zk), group(X.at[1], zk), fsend.at[zk], frecv.at[zk], partner).wait_recv()
-            to_rows(group(X.at[0], zk)[...], XR, i * 48)
-            to_rows(group(X.at[1], zk)[...], XR, 96 + i * 48)
-        if j == 0:
-            for load in loads:
-                load.wait()
-        rows = XR[...]
-        gated, upper = dot(rows, G[...]), dot(rows, U[...])
-        HID[...] = (jax.nn.gelu(gated) * upper).astype(BF)
-        PS[j] = dot(HID[96:, :], DN[...]).astype(BF)
-        swap(j).start()
-        OWN[j] = dot(HID[:96, :], DN[...])
-
-    def back(j, chunk):
-        swap(j).wait()
-        total = (OWN[j] + PX[j].astype(F32)).astype(BF)
-        for i, zk in enumerate(chunk):
-            zi = zt(zk, -1)
-            RB[pl.ds(zi * NX, NX)] = to_blocks(total[i * 48 : (i + 1) * 48])
-            exchange(zi, int(zk == 0), zk, RB, R, rsend, rrecv, -1)
-            if zk == 0:
-                R[here] = RB[here]
-
-    for j in range(len(CHUNKS) + 2):
-        if j < len(CHUNKS):
-            forward(CHUNKS[j])
-        if 1 <= j <= len(CHUNKS):
-            work(j - 1, CHUNKS[j - 1])
-        if j >= 2:
-            back(j - 2, CHUNKS[j - 2])
-
-    expert_c = lax.broadcasted_iota(jnp.int32, (DEC, EXPERTS), 1)
-    hot = [(expert_c == routes[:, k : k + 1]).astype(F32) for k in (0, 1)]
-    count = dot((t1 < t0).astype(BF), (hot[0] + hot[1]).astype(BF))
-    slot_id = lax.broadcasted_iota(jnp.int32, (DEC, SLOTS), 1)
-    picks = []
-    for k in (0, 1):
-        slot = jnp.sum(count * hot[k], axis=1, keepdims=True).astype(jnp.int32)
-        picks.append((slot_id == routes[:, k : k + 1] * CAP + slot).astype(F32).astype(BF))
-
-    for chunk in CHUNKS:
-        for zk in chunk:
-            zi = zt(zk, 1)
-            remote(group(X.at[0], zk), group(X.at[0], zk), fsend.at[zk], frecv.at[zk], partner).wait_send()
-
-            @pl.loop(int(zk == 0), NX)
-            def _(xk):
-                k = zk * NX + xk
-                block = R.at[zi * NX + xt(xk, 1)]
-                remote(block, block, rsend.at[k], rrecv.at[k], partner).wait()
-                remote(block, block, dsend.at[k], drecv.at[k], partner).wait_send()
-
-            to_rows(R[pl.ds(zi * NX, NX)], RR, pl.multiple_of(zi * 48, 16))
-    total = mixed[...].astype(F32)
-    moe = [dot(picks[k], RR[...]) * gates[:, k : k + 1] for k in (0, 1)]
-    out[...] = (total + (moe[0] + moe[1])).astype(BF)
-
-
-def spread_matrix():
-    m = np.zeros((192, 192), np.float32)
-    for s in range(4):
-        for q in range(4):
-            for c in range(CAP):
-                m[s * 48 + q * 12 + c, q * 48 + s * 12 + c] = 1
-    return m
-
-
-def experts(mixed, gain, routes, gates, wg, wu, wd):
-    vmem, hbm = pl.BlockSpec(memory_space=pltpu.VMEM), pl.BlockSpec(memory_space=pl.ANY)
-    spread = spread_matrix()
-    dma = pltpu.SemaphoreType.DMA
-    return pl.pallas_call(
-        moe_kernel,
-        name="experts",
-        out_shape=jax.ShapeDtypeStruct((DEC, D), BF),
-        in_specs=[vmem] * 7 + [hbm] * 3,
-        out_specs=vmem,
-        scratch_shapes=[
+            dma((SEMS_A,)),
+            dma((SEMS_A,)),
             pltpu.VMEM((D, PIECE), BF),
             pltpu.VMEM((D, PIECE), BF),
             pltpu.VMEM((PIECE, D), BF),
@@ -639,7 +632,8 @@
             pltpu.VMEM((32, 48, QUART), BF),
             pltpu.VMEM((32, 48, QUART), BF),
             pltpu.VMEM((SLOTS, D), BF),
-            dma((3,)),
+            pltpu.VMEM((2, SLOTS, DEC), BF),
+            pltpu.VMEM((192, 192), BF),
             dma((32,)),
             dma((32,)),
             dma((8,)),
@@ -648,22 +642,20 @@
             dma((4,)),
             dma((32,)),
             dma((32,)),
+            dma((3,)),
         ],
         compiler_params=pltpu.CompilerParams(
-            collective_id=2, has_side_effects=True, vmem_limit_bytes=56 << 20
+            collective_id=1, has_side_effects=True, vmem_limit_bytes=60 << 20
         ),
-    )(mixed, gain, routes, routes.T, gates, jnp.asarray(spread, BF), jnp.asarray(spread.T, BF), wg, wu, wd)
+    )(prev, enc, wq, wk, wv, wo, gain_attn, gain_moe, routes.T, gates.T, wg, wu, wd)
 
 
 def per_device(previous, encoder_states, routes, gate_values, gain_attn, gain_moe, query_weight,
                key_weight, value_weight, out_weight, expert_gate, expert_up, expert_down):
-    mixed = attention(
+    result = relay(
         previous[0, 0], encoder_states[0], query_weight[0], key_weight[0], value_weight[0],
-        out_weight[0], gain_attn,
-    )
-    result = experts(
-        mixed, gain_moe, routes[0, 0], gate_values[0, 0], expert_gate[0, 0], expert_up[0, 0],
-        expert_down[0, 0],
+        out_weight[0], gain_attn, gain_moe, routes[0, 0], gate_values[0, 0], expert_gate[0, 0],
+        expert_up[0, 0], expert_down[0, 0],
     )
     return result.reshape(previous.shape)
 

time: 138 us -> 126 us (0.913); the launches traced: 136 us -> 126 us
  local copies, waits for them, and re-layouts: 10.9 us -> 1.67 us
    unnamed x18 -> x1, local copies, waits for them, and re-layouts: 9.47 us -> 1.67 us
    squeeze x1 -> x0, local copies, waits for them, and re-layouts: 1.4 us -> none  [per_device(): routes[0, 0]]
    pallas_call x2 -> x1, Pallas kernels: 125 us -> 124 us  [relay(): pl.pallas_call(relay_kernel, name='relay', out_shape=jax.ShapeDtypeStruct...]
where the time goes in v3:
time: 126 us
  Pallas kernels  124 us (98%)
  local copies, waits for them, and re-layouts  1.67 us (1%)
    pallas_call x1, Pallas kernels, relay(): pl.pallas_call(relay_kernel, name='relay', out_shape=jax.ShapeDtypeStruct...  124 us

profile of v3, /device:TPU:16, one launch (start us, length us, event | category | flops | bytes accessed | tf_op | source)
XLA Modules:
  0.0 125.9 jit_solution(12054045464784662593)
XLA Ops:
  0.0 124.2 %relay.1 = bf16[128,1024]{1,0:T(8,128)(2,1)} custom-call(bf16[128,1024]{1,0:T(8,128)(2,1)} %bitcast.21, bf16[256,1024]{1,0:T(8,128)(2,1)} %bitcast.20, bf16[16,1024]{1,0:T(8,128)(2,1)} %bitcast.22, bf16[16,1024]{1,0:T(8,128)(2,1)} %bitcast.23, bf16[16,1024]{1,0:T(8,128)(2,1)} %bitcast.24, bf16[16,1024]{1,0:T(8,128)(2,1)} %bitcast.25, f32[1,1024]{1,0:T(1,128)} %gain_attn.1, ...), custom_call_target="tpu_custom_call" | custom-call | tf_op jit(solution)/shard_map/relay/pallas_call | solution.py:597
  124.2 1.7 %copy.15 = bf16[1,1,128,1024]{3,2,1,0:T(8,128)(2,1)} copy(bf16[1,1,128,1024]{3,2,1,0:T(8,128)(2,1)} %bitcast.19) | data formatting | bytes 524288

commit v4 on v3

--- a/solution.py
+++ b/solution.py
@@ -370,7 +370,7 @@
     lane = lax.broadcasted_iota(jnp.int32, (DEC, 128), 1)
 
     def at(seq):
-        @pl.loop(0, 4)
+        @pl.loop(0, 4, unroll=True)
         def _(pair):
             columns = pl.ds(pl.multiple_of(pair * 128, 128), 128)
             rows = pl.ds(seq * DEC, DEC)
@@ -420,7 +420,7 @@
     return pending
 
 
-CHUNKS = ((1, 5), (3, 7), (2, 6), (0, 4))
+CHUNKS = ((1, 7), (2, 6), (3, 5), (4,), (0,))
 
 
 def experts_part(mixed, gain, routes_t, gates_t, loads, out,
@@ -478,12 +478,16 @@
             k = zk * NX + xk
             remote(src.at[zi * NX + xi], dst.at[here], s.at[k], r.at[k], plane(zi, xi)).start()
 
-    for chunk in CHUNKS:
+    def dispatch(chunk):
         for zk in chunk:
             zi = zt(zk, 1)
             BUF[pl.ds(zi * NX, NX)] = to_blocks(B0[rows_of(zi), :])
             exchange(zi, int(zk == 0), zk, BUF, X.at[0], dsend, drecv, 1)
-    X[0, here] = BUF[here]
+            if zk == 0:
+                X[0, here] = BUF[here]
+
+    for chunk in CHUNKS:
+        dispatch(chunk)
 
     def group(ref, zk):
         return ref.at[pl.ds(zt(zk, -1) * NX, NX)]
@@ -499,30 +503,34 @@
 
             remote(group(X.at[0], zk), group(X.at[1], zk), fsend.at[zk], frecv.at[zk], partner).start()
 
+    def part(j):
+        return pl.ds(sum(len(chunk) for chunk in CHUNKS[:j]), len(CHUNKS[j]))
+
     def swap(j):
-        return remote(PS.at[j], PX.at[j], psend.at[j], precv.at[j], partner)
+        return remote(PS.at[part(j)], PX.at[part(j)], psend.at[j], precv.at[j], partner)
 
     def work(j, chunk):
+        half = 48 * len(chunk)
         for i, zk in enumerate(chunk):
             remote(group(X.at[1], zk), group(X.at[1], zk), fsend.at[zk], frecv.at[zk], partner).wait_recv()
             to_rows(group(X.at[0], zk)[...], XR, i * 48)
-            to_rows(group(X.at[1], zk)[...], XR, 96 + i * 48)
+            to_rows(group(X.at[1], zk)[...], XR, half + i * 48)
         if j == 0:
             for load in loads:
                 load.wait()
-        rows = XR[...]
+        rows = XR[: 2 * half, :]
         gated, upper = dot(rows, G[...]), dot(rows, U[...])
-        HID[...] = (jax.nn.gelu(gated) * upper).astype(BF)
-        PS[j] = dot(HID[96:, :], DN[...]).astype(BF)
+        HID[: 2 * half, :] = (jax.nn.gelu(gated) * upper).astype(BF)
+        PS[part(j)] = dot(HID[half : 2 * half, :], DN[...]).astype(BF).reshape(len(chunk), 48, D)
         swap(j).start()
-        OWN[j] = dot(HID[:96, :], DN[...])
+        OWN[part(j)] = dot(HID[:half, :], DN[...]).reshape(len(chunk), 48, D)
 
     def back(j, chunk):
         swap(j).wait()
-        total = (OWN[j] + PX[j].astype(F32)).astype(BF)
+        total = (OWN[part(j)] + PX[part(j)].astype(F32)).astype(BF)
         for i, zk in enumerate(chunk):
             zi = zt(zk, -1)
-            RB[pl.ds(zi * NX, NX)] = to_blocks(total[i * 48 : (i + 1) * 48])
+            RB[pl.ds(zi * NX, NX)] = to_blocks(total[i])
             exchange(zi, int(zk == 0), zk, RB, R, rsend, rrecv, -1)
             if zk == 0:
                 R[here] = RB[here]
@@ -626,9 +634,9 @@
             pltpu.VMEM((2, 32, 48, QUART), BF),
             pltpu.VMEM((192, D), BF),
             pltpu.VMEM((192, PIECE), BF),
-            pltpu.VMEM((4, 96, D), F32),
-            pltpu.VMEM((4, 96, D), BF),
-            pltpu.VMEM((4, 96, D), BF),
+            pltpu.VMEM((8, 48, D), F32),
+            pltpu.VMEM((8, 48, D), BF),
+            pltpu.VMEM((8, 48, D), BF),
             pltpu.VMEM((32, 48, QUART), BF),
             pltpu.VMEM((32, 48, QUART), BF),
             pltpu.VMEM((SLOTS, D), BF),
@@ -638,8 +646,8 @@
             dma((32,)),
             dma((8,)),
             dma((8,)),
-            dma((4,)),
-            dma((4,)),
+            dma((8,)),
+            dma((8,)),
             dma((32,)),
             dma((32,)),
             dma((3,)),

time: 126 us -> 123 us (0.976)
  Pallas kernels: 124 us -> 122 us
    pallas_call x1, Pallas kernels: 124 us -> 122 us  [relay(): pl.pallas_call(relay_kernel, name='relay', out_shape=jax.ShapeDtypeStruct...]
where the time goes in v4:
time: 123 us
  Pallas kernels  122 us (99%)
  local copies, waits for them, and re-layouts  1.67 us (1%)
    pallas_call x1, Pallas kernels, relay(): pl.pallas_call(relay_kernel, name='relay', out_shape=jax.ShapeDtypeStruct...  122 us

profile of v4, /device:TPU:16, one launch (start us, length us, event | category | flops | bytes accessed | tf_op | source)
XLA Modules:
  0.0 123.3 jit_solution(17709639622896902494)
XLA Ops:
  0.0 121.6 %relay.1 = bf16[128,1024]{1,0:T(8,128)(2,1)} custom-call(bf16[128,1024]{1,0:T(8,128)(2,1)} %bitcast.21, bf16[256,1024]{1,0:T(8,128)(2,1)} %bitcast.20, bf16[16,1024]{1,0:T(8,128)(2,1)} %bitcast.22, bf16[16,1024]{1,0:T(8,128)(2,1)} %bitcast.23, bf16[16,1024]{1,0:T(8,128)(2,1)} %bitcast.24, bf16[16,1024]{1,0:T(8,128)(2,1)} %bitcast.25, f32[1,1024]{1,0:T(1,128)} %gain_attn.1, ...), custom_call_target="tpu_custom_call" | custom-call | tf_op jit(solution)/shard_map/relay/pallas_call | solution.py:605
  121.6 1.7 %copy.15 = bf16[1,1,128,1024]{3,2,1,0:T(8,128)(2,1)} copy(bf16[1,1,128,1024]{3,2,1,0:T(8,128)(2,1)} %bitcast.19) | data formatting | bytes 524288

commit v5 on v4

--- a/solution.py
+++ b/solution.py
@@ -423,7 +423,7 @@
 CHUNKS = ((1, 7), (2, 6), (3, 5), (4,), (0,))
 
 
-def experts_part(mixed, gain, routes_t, gates_t, loads, out,
+def experts_part(mixed, gain, gates_t, loads, out,
                  G, U, DN, B0, BUF, X, XR, HID, OWN, PS, PX, RB, R, RR, PK, SP,
                  dsend, drecv, fsend, frecv, psend, precv, rsend, rrecv):
     z, x, y, b = place_of()
@@ -455,16 +455,6 @@
             dst[pl.ds(first, 48), q * QUART : (q + 1) * QUART] = stacked[q * 48 : (q + 1) * 48]
 
     moe_in = rms(mixed.astype(F32), gain[...]).astype(BF)
-    expert_r = lax.broadcasted_iota(jnp.int32, (EXPERTS, DEC), 0)
-    hot = [(expert_r == routes_t[k : k + 1, :]).astype(F32) for k in (0, 1)]
-    t0 = lax.broadcasted_iota(jnp.int32, (DEC, DEC), 0)
-    t1 = lax.broadcasted_iota(jnp.int32, (DEC, DEC), 1)
-    count = dot((hot[0] + hot[1]).astype(BF), (t0 < t1).astype(BF))
-    slot_id = lax.broadcasted_iota(jnp.int32, (SLOTS, DEC), 0)
-    for k in (0, 1):
-        slot = jnp.sum(count * hot[k], axis=0, keepdims=True).astype(jnp.int32)
-        position = routes_t[k : k + 1, :] * CAP + slot
-        PK[k] = (slot_id == position).astype(F32).astype(BF)
     place = PK[0] + PK[1]
     B0[...] = dot(place, moe_in).astype(BF)
 
@@ -568,6 +558,19 @@
     out[...] = (mixed.astype(F32) + (moe[0] + moe[1])).astype(BF)
 
 
+def slot_rows(routes_t, PK):
+    expert_r = lax.broadcasted_iota(jnp.int32, (EXPERTS, DEC), 0)
+    hot = [(expert_r == routes_t[k : k + 1, :]).astype(F32) for k in (0, 1)]
+    t0 = lax.broadcasted_iota(jnp.int32, (DEC, DEC), 0)
+    t1 = lax.broadcasted_iota(jnp.int32, (DEC, DEC), 1)
+    count = dot((hot[0] + hot[1]).astype(BF), (t0 < t1).astype(BF))
+    slot_id = lax.broadcasted_iota(jnp.int32, (SLOTS, DEC), 0)
+    for k in (0, 1):
+        slot = jnp.sum(count * hot[k], axis=0, keepdims=True).astype(jnp.int32)
+        position = routes_t[k : k + 1, :] * CAP + slot
+        PK[k] = (slot_id == position).astype(F32).astype(BF)
+
+
 def swap_matrix():
     row = lax.broadcasted_iota(jnp.int32, (192, 192), 0)
     column = lax.broadcasted_iota(jnp.int32, (192, 192), 1)
@@ -587,6 +590,7 @@
 
     def load():
         second[15][...] = swap_matrix()
+        slot_rows(routes_t, second[14])
         for copy in loads:
             copy.start()
 
@@ -594,7 +598,7 @@
         PLAN, prev, enc, wq, wk, wv, wo, gain_attn, *first, load
     )
     mixed = jnp.concatenate([H[0], H[1]], axis=1)
-    experts_part(mixed, gain_moe, routes_t, gates_t, loads, out, *second)
+    experts_part(mixed, gain_moe, gates_t, loads, out, *second)
     for wait in pending:
         wait()
 

time: 123 us -> 123 us (level)
  no operation moved by 1% of the time
where the time goes in v5:
time: 123 us
  Pallas kernels  122 us (99%)
  local copies, waits for them, and re-layouts  1.67 us (1%)
    pallas_call x1, Pallas kernels, relay(): pl.pallas_call(relay_kernel, name='relay', out_shape=jax.ShapeDtypeStruct...  122 us

profile of v5, /device:TPU:16, one launch (start us, length us, event | category | flops | bytes accessed | tf_op | source)
XLA Modules:
  0.0 123.2 jit_solution(13055198631737925632)
XLA Ops:
  0.0 121.5 %relay.1 = bf16[128,1024]{1,0:T(8,128)(2,1)} custom-call(bf16[128,1024]{1,0:T(8,128)(2,1)} %bitcast.21, bf16[256,1024]{1,0:T(8,128)(2,1)} %bitcast.20, bf16[16,1024]{1,0:T(8,128)(2,1)} %bitcast.22, bf16[16,1024]{1,0:T(8,128)(2,1)} %bitcast.23, bf16[16,1024]{1,0:T(8,128)(2,1)} %bitcast.24, bf16[16,1024]{1,0:T(8,128)(2,1)} %bitcast.25, f32[1,1024]{1,0:T(1,128)} %gain_attn.1, ...), custom_call_target="tpu_custom_call" | custom-call | tf_op jit(solution)/shard_map/relay/pallas_call | solution.py:609
  121.5 1.7 %copy.15 = bf16[1,1,128,1024]{3,2,1,0:T(8,128)(2,1)} copy(bf16[1,1,128,1024]{3,2,1,0:T(8,128)(2,1)} %bitcast.19) | data formatting | bytes 524288
